TPU v7x, 512 devices: a whole 4x8x8 slice. The times are simulated.
512 devices in a mesh: fsdp: 64 (over x, y, core), tp: 8 (over z).
Axes of the slice: x: 4, y: 8, z: 8, core: 2. Of those that a mesh axis runs over, the one named last changes fastest.
Arguments:
- mom_up: float32 [3072, 12288], P('fsdp', 'tp'), may hold values from -6 to 6
- grad_up: bfloat16 [3072, 12288], P('fsdp', 'tp'), may hold values from -150 to 150
- basis_up: float32 [8, 1536, 256], P('tp', 'fsdp'), may hold values from -6 to 6
- mom_down: float32 [12288, 3072], P('fsdp', 'tp'), may hold values from -6 to 6
- grad_down: bfloat16 [12288, 3072], P('fsdp', 'tp'), may hold values from -150 to 150
- basis_down: float32 [8, 384, 256], P('tp', 'fsdp'), may hold values from -6 to 6
Outputs:
- update_up: float32 [3072, 12288], P('fsdp', 'tp')
- next_mom_up: float32 [3072, 12288], P('fsdp', 'tp')
- next_basis_up: float32 [8, 1536, 256], P('tp', 'fsdp')
- update_down: float32 [12288, 3072], P('fsdp', 'tp')
- next_mom_down: float32 [12288, 3072], P('fsdp', 'tp')
- next_basis_down: float32 [8, 384, 256], P('tp', 'fsdp')
All inputs are finite; a program needn't handle non-finite values.
Results may differ from a plain program's by a relative error of at most 0.00055.
Values sent between devices are 32-bit elements; how exact they have to be, the bound alone decides.
A program may use at most 64 MiB of HBM per device.

v0:
```python
import math

import jax
import jax.numpy as jnp
from jax import lax
from jax.sharding import PartitionSpec as P

retain = 0.9
epsilon = 1e-06
HIGH = lax.Precision.HIGHEST


def folded(piece, axis, dim, hop, start):

    def gathered(part):
        return lax.all_gather(part, axis, axis=dim, tiled=True)

    return hop(start, jax.tree.map(gathered, piece), jnp.int32(0))


def add_columns(source, piece):
    return jnp.dot(source, piece[0], precision=HIGH, preferred_element_type=jnp.float32)


def contract_rows(left, right_side):
    return lax.dot_general(
        left,
        right_side,
        (((0,), (0,)), ((), ())),
        precision=HIGH,
        preferred_element_type=jnp.float32,
    )


def outer_rows(left, right_side):
    return lax.dot_general(
        left,
        right_side,
        (((1,), (1,)), ((), ())),
        precision=HIGH,
        preferred_element_type=jnp.float32,
    )


def body(mom_up, grad_up, basis_up, mom_down, grad_down, basis_down):
    matrices = ((mom_up, grad_up, basis_up), (mom_down, grad_down, basis_down))
    width = basis_up.shape[2]
    blended = [moment + gradient.astype(jnp.float32) for moment, gradient, _ in matrices]
    partials = []
    for which in range(2):
        source = blended[which]
        init = jnp.zeros((source.shape[0], width), jnp.float32)
        partials.append(
            folded(
                matrices[which][2],
                "fsdp",
                1,
                lambda total, piece, start, source=source: add_columns(source, piece),
                init,
            )
        )
    projected = [lax.psum(term, "tp") for term in partials]
    local_grams = [contract_rows(rows_part, rows_part) for rows_part in projected]
    grams = [lax.psum(square, "fsdp") for square in local_grams]
    outputs = []
    for which in range(2):
        moment, gradient, basis = matrices[which]
        source = blended[which]
        lower = jnp.linalg.cholesky(grams[which])
        ortho = lax.linalg.triangular_solve(
            lower, projected[which], left_side=False, lower=True, transpose_a=True
        )
        right_term = contract_rows(source, ortho)
        local_rows = basis.shape[1]
        total_cols = source.shape[1] * lax.axis_size("tp")
        total_rows = source.shape[0] * lax.axis_size("fsdp")
        right = lax.psum(right_term, "fsdp")
        sums = lax.psum(jnp.sum(right * right, axis=0), "tp")
        scale = lax.rsqrt(sums + epsilon)
        owned = lax.dynamic_slice_in_dim(right, lax.axis_index("fsdp") * local_rows, local_rows, 0)
        next_basis = (owned * scale[None, :]).reshape(basis.shape)
        full_basis = right * scale[None, :]
        next_mom = source - (1.0 - retain) * outer_rows(ortho, right)
        update = math.sqrt(total_rows / total_cols) * outer_rows(ortho, full_basis)
        outputs.extend([update, next_mom, next_basis])
    return tuple(outputs)


def solution(mesh):
    return jax.shard_map(
        body,
        mesh=mesh,
        in_specs=(
            P("fsdp", "tp"),
            P("fsdp", "tp"),
            P("tp", "fsdp", None),
            P("fsdp", "tp"),
            P("fsdp", "tp"),
            P("tp", "fsdp", None),
        ),
        out_specs=(
            P("fsdp", "tp"),
            P("fsdp", "tp"),
            P("tp", "fsdp", None),
            P("fsdp", "tp"),
            P("fsdp", "tp"),
            P("tp", "fsdp", None),
        ),
        check_vma=False,
    )
```

profile of v0, /device:TPU:1, one launch (start us, length us, event | category | flops | bytes accessed | tf_op | source)
XLA Modules:
  0.0 726.5 jit_solution(11063102039122834986)
XLA Ops:
  8.1 50.8 %all_gather.7 = f32[1,384,256]{2,0,1:T(1,128)S(1)} all-gather(f32[1,6,256]{2,0,1:T(1,128)} %param.12), channel_id=1, replica_groups=mesh['fsdp'=64,'tp'=8] {'fsdp'}, dimensions={1}, use_global_device_ids=true | all-gather | bytes 399360 | tf_op jit(solution)/shard_map/all_gather | solution.py:16
  58.9 2.2 fusion.6
  61.1 0.5 all-gather.2.cloned.1.call-update
  61.7 73.3 %all-reduce.8.cloned.1.call-done = f32[192,256]{1,0:T(8,128)} async-done(((f32[192,256]{1,0:T(8,128)}), f32[192,256]{1,0:T(8,128)}) %all-reduce.8.cloned.1.call-update) | async-done | bytes 196624 | tf_op jit(solution)/shard_map/psum | solution.py:62
  135.0 2.4 fusion.38
  137.4 9.5 %all-gather.2.cloned.1.call-done = f32[1,1536,256]{2,1,0:T(8,128)} async-done(((f32[1,24,256]{2,1,0:T(8,128)}), f32[1,1536,256]{2,1,0:T(8,128)}) %all-gather.2.cloned.1.call-update) | async-done | bytes 1572880 | tf_op jit(solution)/shard_map/all_gather | solution.py:16
  146.9 2.3 fusion.1
  149.2 24.1 %psum.56 = f32[48,256]{1,0:T(8,128)S(1)} all-reduce(f32[48,256]{1,0:T(8,128)S(1)} %fusion.1), channel_id=1, replica_groups=mesh['fsdp'=64,'tp'=8] {'tp'}, use_global_device_ids=true, to_apply=%region_0.0 | all-reduce | flops 12288 | bytes 98304 | tf_op jit(solution)/shard_map/psum | solution.py:62
  173.3 1.1 fusion.37
  174.4 0.5 all-reduce.10.cloned.1.call-start
  175.0 192.1 %all-reduce.12.cloned.1.call-done = (f32[256,256]{0,1:T(8,128)}, f32[256,256]{0,1:T(8,128)}) async-done(((f32[256,256]{0,1:T(8,128)}, f32[256,256]{0,1:T(8,128)}), (f32[256,256]{0,1:T(8,128)}, f32[256,256]{0,1:T(8,128)})) %all-reduce.12.cloned.1.call-update) | async-done | bytes 524304 | tf_op jit(solution)/shard_map/psum | solution.py:64
  367.1 1.1 copy.18
  368.2 1.1 copy.20
  369.3 1.1 fusion.10
  370.4 11.7 %cholesky.164 = f32[128,128]{1,0:T(8,128)S(1)} custom-call(f32[128,128]{1,0:T(8,128)S(1)} %cholesky.197), custom_call_target="Cholesky" | custom-call | tf_op jit(solution)/shard_map/jit(cholesky)/cholesky | solution.py:69
  382.1 9.8 %custom-call.18 = f32[1,128,128]{1,2,0:T(8,128)S(1)} custom-call(f32[1,128,128]{2,1,0:T(8,128)S(1)} %get-tuple-element.64), custom_call_target="InvertDiagBlocksLowerTriangular" | custom-call | tf_op jit(solution)/shard_map/jit(cholesky)/cholesky | solution.py:69
  392.5 11.7 %cholesky.181 = f32[128,128]{1,0:T(8,128)S(1)} custom-call(f32[128,128]{1,0:T(8,128)S(1)} %convolution_subtract_fusion.1), custom_call_target="Cholesky" | custom-call | tf_op jit(solution)/shard_map/jit(cholesky)/cholesky | solution.py:69
  404.2 0.6 compare_reduce_fusion
  404.9 0.6 compare_reduce_fusion.1
  406.9 4.0 while.3
  407.0 0.6 fusion.56
  407.5 1.4 bitcast_dynamic-update-slice_fusion.5
  409.0 0.6 fusion.56
  409.5 1.4 bitcast_dynamic-update-slice_fusion.5
  410.9 19.8 %custom-call.15 = f32[2,128,128]{1,2,0:T(8,128)S(1)} custom-call(f32[2,128,128]{2,1,0:T(8,128)S(1)} %get-tuple-element.22), custom_call_target="InvertDiagBlocksLowerTriangular" | custom-call | tf_op jit(solution)/shard_map/triangular_solve | solution.py:70
  431.0 0.3 convolution_subtract_fusion
  431.6 1.6 fusion.13
  433.2 11.7 %cholesky.130 = f32[128,128]{1,0:T(8,128)S(1)} custom-call(f32[128,128]{1,0:T(8,128)S(1)} %cholesky.194), custom_call_target="Cholesky" | custom-call | tf_op jit(solution)/shard_map/jit(cholesky)/cholesky | solution.py:69
  444.9 9.8 %custom-call.17 = f32[1,128,128]{1,2,0:T(8,128)S(1)} custom-call(f32[1,128,128]{2,1,0:T(8,128)S(1)} %get-tuple-element.68), custom_call_target="InvertDiagBlocksLowerTriangular" | custom-call | tf_op jit(solution)/shard_map/jit(cholesky)/cholesky | solution.py:69
  455.3 11.7 %cholesky.147 = f32[128,128]{1,0:T(8,128)S(1)} custom-call(f32[128,128]{1,0:T(8,128)S(1)} %convolution_subtract_fusion.2), custom_call_target="Cholesky" | custom-call | tf_op jit(solution)/shard_map/jit(cholesky)/cholesky | solution.py:69
  467.0 0.6 compare_reduce_fusion.2
  467.7 0.6 compare_reduce_fusion.3
  469.6 4.0 while.2
  469.7 0.6 fusion.55
  470.3 1.4 bitcast_dynamic-update-slice_fusion.4
  471.7 0.6 fusion.55
  472.3 1.4 bitcast_dynamic-update-slice_fusion.4
  473.7 19.9 %custom-call.14 = f32[2,128,128]{1,2,0:T(8,128)S(1)} custom-call(f32[2,128,128]{2,1,0:T(8,128)S(1)} %get-tuple-element.14), custom_call_target="InvertDiagBlocksLowerTriangular" | custom-call | tf_op jit(solution)/shard_map/triangular_solve | solution.py:70
  494.1 2.6 fusion.14
  496.8 196.8 %all-reduce.10.cloned.1.call-done = (f32[1536,256]{1,0:T(8,128)}, f32[384,256]{1,0:T(8,128)}) async-done(((f32[1536,256]{1,0:T(8,128)}, f32[384,256]{1,0:T(8,128)}), (f32[1536,256]{1,0:T(8,128)}, f32[384,256]{1,0:T(8,128)})) %all-reduce.10.cloned.1.call-update) | async-done | bytes 1966096 | tf_op jit(solution)/shard_map/psum | solution.py:77
  693.6 1.2 multiply_reduce_fusion.1
  694.8 2.3 fusion.4
  697.3 2.3 fusion
  699.5 14.3 %all-reduce.3 = (f32[256]{0:T(256)S(1)}, f32[256]{0:T(256)S(1)}) all-reduce(f32[256]{0:T(256)S(1)} %multiply_reduce_fusion, f32[256]{0:T(256)S(1)} %multiply_reduce_fusion.1), channel_id=1, replica_groups=mesh['fsdp'=64,'tp'=8] {'tp'}, use_global_device_ids=true, to_apply=%region_8.0 | all-reduce | flops 512 | bytes 4096 | tf_op jit(solution)/shard_map/psum | solution.py:78
  713.9 1.3 convolution_multiply_fusion.3
  715.2 0.6 copy.21
  715.8 2.2 convolution_multiply_fusion.1
  718.0 0.6 multiply_bitcast_fusion
  (51 shorter events, 2.8 us)
Async XLA Ops:
  8.0 138.9 %copy-start.2 = (f32[48,1536]{1,0:T(8,128)S(1)}, f32[48,1536]{1,0:T(8,128)}, u32[]{:S(2)}) copy-start(f32[48,1536]{1,0:T(8,128)} %param.7) | copy-start | bytes 884740
  8.0 138.9 %copy-start.5 = (bf16[48,1536]{1,0:T(8,128)(2,1)S(1)}, bf16[48,1536]{1,0:T(8,128)(2,1)}, u32[]{:S(2)}) copy-start(bf16[48,1536]{1,0:T(8,128)(2,1)} %param.8) | copy-start | bytes 442372
  8.0 126.9 %all-reduce.8.cloned.1.call-start = ((), (), s32[]{:S(2)}) async-start(), calls=%async_computation.1 | async-start | bytes 393216 | tf_op jit(solution)/shard_map/psum | solution.py:62
  61.0 85.8 %all-gather.2.cloned.1.call-start = ((), (), s32[]{:S(2)}) async-start(), calls=%async_computation | async-start | bytes 1597440 | tf_op jit(solution)/shard_map/all_gather | solution.py:16
  61.6 305.5 %all-reduce.12.cloned.1.call-start = ((), (), s32[]{:S(2)}) async-start(), calls=%async_computation.3 | async-start | bytes 1048576 | tf_op jit(solution)/shard_map/psum | solution.py:64
  174.4 519.2 %all-reduce.10.cloned.1.call-start = ((), (), s32[]{:S(2)}) async-start(), calls=%async_computation.2 | async-start | bytes 3932160 | tf_op jit(solution)/shard_map/psum | solution.py:77
  370.4 60.4 %copy-start.4 = (f32[192,256]{1,0:T(8,128)S(1)}, f32[192,256]{1,0:T(8,128)}, u32[]{:S(2)}) copy-start(f32[192,256]{1,0:T(8,128)} %all-reduce.8.cloned.1.call-done) | copy-start | bytes 589828
  392.0 39.6 %copy-start.3 = (f32[192,384]{1,0:T(8,128)S(1)}, f32[192,384]{1,0:T(8,128)}, u32[]{:S(2)}) copy-start(f32[192,384]{1,0:T(8,128)} %param.10) | copy-start | bytes 884740
  392.0 39.6 %copy-start.6 = (bf16[192,384]{1,0:T(8,128)(2,1)S(1)}, bf16[192,384]{1,0:T(8,128)(2,1)}, u32[]{:S(2)}) copy-start(bf16[192,384]{1,0:T(8,128)(2,1)} %param.11) | copy-start | bytes 442372
  693.6 3.4 copy-start
  697.3 16.6 %copy-start.1 = (f32[384,256]{1,0:T(8,128)S(1)}, f32[384,256]{1,0:T(8,128)}, u32[]{:S(2)}) copy-start(f32[384,256]{1,0:T(8,128)} %get-tuple-element.52) | copy-start | bytes 1179652
Sparse Core Ops, SparseCore 0:
  61.2 73.7 all-reduce.7
Sparse Core Ops, SparseCore 1:
  64.9 82.0 all-gather.1
  174.5 192.5 all-reduce.11
  496.8 196.7 all-reduce.9
where the time goes:
time: 735 us; the launch traced here: 726 us
  waiting for transfers between devices  472 us (64%)
  other arithmetic  112 us (15%)
  blocking collectives  89.2 us (12%)
  matrix products  22.5 us (3%)
  between operations  18.8 us (3%)
  local copies, waits for them, and re-layouts  10.8 us (1%)
    psum x1, waiting for transfers between devices, body(): right = lax.psum(right_term, 'fsdp')  197 us
    psum x1, waiting for transfers between devices, body(): grams = [lax.psum(square, 'fsdp') for square in local_grams]  192 us
    psum x1, waiting for transfers between devices, body(): projected = [lax.psum(term, 'tp') for term in partials]  73.3 us
    another operation x14, other arithmetic, body(): lower = jnp.linalg.cholesky(grams[which])  69.2 us
    all_gather x1, blocking collectives, gathered(): return lax.all_gather(part, axis, axis=dim, tiled=True)  50.8 us
    another operation x5, other arithmetic, body(): lax.linalg.triangular_solve(lower, projected[which], left_side=False, low...  39.8 us
    psum x1, blocking collectives, body(): projected = [lax.psum(term, 'tp') for term in partials]  24.1 us
  transfers between devices with their start and end apart: 4, of which 4 were waited for; matrix products, arithmetic and copies ran while one was open for 0% of the time, Pallas kernels for 0%

commit v1 on v0

v1 whole, which is shorter than its diff:
```python
import math

import jax
import jax.numpy as jnp
from jax import lax
from jax.experimental import pallas as pl
from jax.experimental.pallas import tpu as pltpu
from jax.sharding import PartitionSpec as P

retain = 0.9
epsilon = 1e-06
HIGH = lax.Precision.HIGHEST
MESH = pl.DeviceIdType.MESH
NX, NY, NZ, RANK = 4, 8, 8, 256
F32 = jnp.float32


def dot(a, b, ca=1, cb=0):
    return lax.dot_general(
        a, b, (((ca,), (cb,)), ((), ())), precision=HIGH, preferred_element_type=F32
    )


def invert_half(a):
    lanes = lax.broadcasted_iota(jnp.int32, (8, 128), 1)
    subs = lax.broadcasted_iota(jnp.int32, (8, 128), 0)
    groups = [a[8 * g : 8 * g + 8] for g in range(16)]
    done = []
    for k in range(16):
        base = 8 * k
        inside = (lanes >= base) & (lanes < base + 8)
        panel = groups[0]
        cols = [jnp.broadcast_to(panel[:, base + j : base + j + 1], (8, 128)) for j in range(8)]
        held = jnp.where(inside, (lanes == subs + base).astype(F32), panel)
        pivots = cols[0]
        inverse, heads = [], []
        for j in range(8):
            r = 1.0 / cols[j][j : j + 1]
            inverse.append(r)
            mult = jnp.where(subs > j, cols[j] * r, 0.0)
            heads.append([c[j : j + 1] for c in cols])
            for jj in range(j + 1, 8):
                cols[jj] = cols[jj] - mult * heads[j][jj]
            held = held - mult * held[j : j + 1]
            if j:
                pivots = jnp.where(subs == j, cols[j], pivots)
        done.append(jnp.where(lanes <= subs + base, held * lax.rsqrt(pivots), 0.0))
        rest = []
        for g in groups[1:]:
            c = [jnp.broadcast_to(g[:, base + j : base + j + 1], (8, 128)) for j in range(8)]
            out = jnp.where(inside, 0.0, g)
            for j in range(8):
                m = c[j] * inverse[j]
                for jj in range(j + 1, 8):
                    c[jj] = c[jj] - m * heads[j][jj]
                out = out - m * held[j : j + 1]
            rest.append(out)
        groups = rest
    return jnp.concatenate(done, axis=0)


def place():
    f = lax.axis_index("fsdp")
    return f // 16, lax.rem(f // 2, 8), lax.rem(f, 2), lax.axis_index("tp")


def kernel(
    mom_up, grad_up, basis_up, mom_down, grad_down, basis_down,
    upd_up, new_up, nb_up, upd_down, new_down, nb_down,
    q, blend_up, blend_down, padded,
    part, part_in, pfull,
    gram, gram_in, gsum, g_x, g_xs, g_y, g_all,
    wpart, wcore, wsum, wu_x, wu_s, wu_y, wd_y, wd_s, wd_x, wfull,
    xinv, ssum, ssum_in,
    send, recv,
):
    x, y, c, z = place()
    count = [0]

    def at(xx, yy, cc, zz):
        return (xx * 16 + yy * 2 + cc, zz)

    def along_y(d):
        return at(x, lax.rem(y + d, NY), c, z)

    def along_x(d):
        return at(lax.rem(x + d, NX), y, c, z)

    def along_z(d):
        return at(x, y, c, lax.rem(z + d, NZ))

    sibling = at(x, y, 1 - c, z)

    barrier = pltpu.get_barrier_semaphore()
    peers = (
        [along_y(d) for d in range(1, NY)]
        + [along_x(d) for d in range(1, NX)]
        + [along_z(d) for d in range(1, NZ)]
        + [sibling]
    )
    for peer in peers:
        pl.semaphore_signal(barrier, inc=1, device_id=peer, device_id_type=MESH)

    started = []

    def transfer(src, dst, device, arrives):
        n = count[0]
        count[0] += 1
        copy = pltpu.make_async_remote_copy(
            src, dst, send.at[n], recv.at[n], device_id=device, device_id_type=MESH
        )
        copy.start()
        started.append(copy)
        landing = pltpu.make_async_remote_copy(
            src, arrives, send.at[n], recv.at[n], device_id=device, device_id_type=MESH
        )
        return landing.wait_recv

    def wait(waits):
        for w in waits:
            w()

    def back(v, d, n):
        return lax.rem(v + n - d, n)

    q[x, y, c, 0:24, :] = basis_up[0]
    q[x, y, c, 24:32, :] = jnp.zeros((8, RANK), F32)
    q[x, y, c, 24:30, :] = basis_down[0]
    pl.semaphore_wait(barrier, len(peers))

    def gather_start(buf):
        up_y = [
            transfer(buf.at[x, y, c, 0:24], buf.at[x, y, c, 0:24], along_y(d),
                     buf.at[x, back(y, d, NY), c, 0:24])
            for d in range(1, NY)
        ]
        down_x = [
            transfer(buf.at[x, y, c, 24:32], buf.at[x, y, c, 24:32], along_x(d),
                     buf.at[back(x, d, NX), y, c, 24:32])
            for d in range(1, NX)
        ]
        return up_y, down_x

    def gather_end(buf, up_y, down_x):
        wait(down_x)
        down_y = [
            transfer(buf.at[:, y, c, 24:32], buf.at[:, y, c, 24:32], along_y(d),
                     buf.at[:, back(y, d, NY), c, 24:32])
            for d in range(1, NY)
        ]
        wait(up_y)
        up_x = [
            transfer(buf.at[x, :, c, 0:24], buf.at[x, :, c, 0:24], along_x(d),
                     buf.at[back(x, d, NX), :, c, 0:24])
            for d in range(1, NX)
        ]
        wait(down_y)
        wait(up_x)
        wait([transfer(buf.at[:, :, c], buf.at[:, :, c], sibling, buf.at[:, :, 1 - c])])

    first = gather_start(q)
    blend_up[...] = mom_up[...] + grad_up[...].astype(F32)
    blend_down[...] = mom_down[...] + grad_down[...].astype(F32)
    column = lax.broadcasted_iota(jnp.int32, (384, 512), 0)
    slot = lax.broadcasted_iota(jnp.int32, (384, 512), 1)
    pick = ((column == (slot // 8) * 6 + lax.rem(slot, 8)) & (lax.rem(slot, 8) < 6)).astype(F32)
    padded[...] = dot(blend_down[...], pick)
    gather_end(q, *first)

    p_up = dot(blend_up[...], q[:, :, :, 0:24, :].reshape(1536, RANK))
    p_down = dot(padded[...], q[:, :, :, 24:32, :].reshape(512, RANK))
    part[:, 0:24, :] = p_down.reshape(8, 24, RANK)
    part[0:6, 24:32, :] = p_up.reshape(6, 8, RANK)
    part[6:8, 24:32, :] = jnp.zeros((2, 8, RANK), F32)
    wait([
        transfer(part.at[lax.rem(z + d, NZ)], part_in.at[d - 1], along_z(d), part_in.at[d - 1])
        for d in range(1, NZ)
    ])
    total = part[z]
    for d in range(1, NZ):
        total = total + part_in[d - 1]
    pfull[z] = total
    wait([
        transfer(pfull.at[z], pfull.at[z], along_z(d), pfull.at[back(z, d, NZ)])
        for d in range(1, NZ)
    ])
    p_up = pfull[0:6, 24:32, :].reshape(48, RANK)
    p_down = pfull[:, 0:24, :].reshape(192, RANK)

    gram[0] = dot(p_up, p_up, 0, 0)
    gram[1] = dot(p_down, p_down, 0, 0)
    gram_wait = transfer(gram.at[1 - c], gram_in, sibling, gram_in)
    wpart[:, :, :, 0:24, :] = dot(blend_up[...], p_up, 0, 0).reshape(NX, NY, 2, 24, RANK)
    wpart[:, :, :, 24:32, :] = dot(padded[...], p_down, 0, 0).reshape(NX, NY, 2, 8, RANK)
    gram_wait()
    gsum[...] = (gram[c] + gram_in[...]).reshape(NX, 64, RANK)
    wait([
        transfer(gsum.at[lax.rem(x + d, NX)], g_x.at[d - 1], along_x(d), g_x.at[d - 1])
        for d in range(1, NX)
    ])
    g_xs[...] = (gsum[x] + g_x[0] + g_x[1] + g_x[2]).reshape(NY, 8, RANK)
    wait([
        transfer(g_xs.at[lax.rem(y + d, NY)], g_y.at[d - 1], along_y(d), g_y.at[d - 1])
        for d in range(1, NY)
    ])
    row = g_xs[y]
    for d in range(1, NY):
        row = row + g_y[d - 1]
    g_all[x, y] = row
    wait([
        transfer(g_all.at[x, y], g_all.at[x, y], along_y(d), g_all.at[x, back(y, d, NY)])
        for d in range(1, NY)
    ])
    g_wait = [
        transfer(g_all.at[x], g_all.at[x], along_x(d), g_all.at[back(x, d, NX)])
        for d in range(1, NX)
    ]

    core_wait = transfer(wpart.at[:, :, 1 - c], wcore, sibling, wcore)
    core_wait()
    wsum[...] = wpart[:, :, c] + wcore[...]
    wait(g_wait)
    up_x = [
        transfer(wsum.at[lax.rem(x + d, NX), :, 0:24], wu_x.at[d - 1], along_x(d), wu_x.at[d - 1])
        for d in range(1, NX)
    ]
    down_y = [
        transfer(wsum.at[:, lax.rem(y + d, NY), 24:32], wd_y.at[d - 1], along_y(d), wd_y.at[d - 1])
        for d in range(1, NY)
    ]

    g11, g12, g22 = (
        g_all[0:2, :, :, 0:128].reshape(128, 128),
        g_all[0:2, :, :, 128:256].reshape(128, 128),
        g_all[2:4, :, :, 128:256].reshape(128, 128),
    )
    x11 = invert_half(g11)
    xinv[c, 0:128, 0:128] = x11
    xinv[c, 0:128, 128:256] = jnp.zeros((128, 128), F32)
    u = dot(x11, g12)
    low = g22 - dot(u, u, 0, 0)
    corner = dot(u, x11, 0, 0)

    wait(up_x)
    wu_s[...] = wsum[x, :, 0:24] + wu_x[0] + wu_x[1] + wu_x[2]
    up_y = [
        transfer(wu_s.at[lax.rem(y + d, NY)], wu_y.at[d - 1], along_y(d), wu_y.at[d - 1])
        for d in range(1, NY)
    ]
    wait(down_y)
    owned = wsum[:, y, 24:32]
    for d in range(1, NY):
        owned = owned + wd_y[d - 1]
    wd_s[...] = owned
    down_x = [
        transfer(wd_s.at[lax.rem(x + d, NX)], wd_x.at[d - 1], along_x(d), wd_x.at[d - 1])
        for d in range(1, NX)
    ]

    x22 = invert_half(low)
    xinv[c, 128:256, 128:256] = x22
    xinv[c, 128:256, 0:128] = -dot(x22, corner)
    x_wait = transfer(xinv.at[c], xinv.at[c], sibling, xinv.at[1 - c])

    wait(up_y)
    owned = wu_s[y]
    for d in range(1, NY):
        owned = owned + wu_y[d - 1]
    wfull[x, y, c, 0:24, :] = owned
    wait(down_x)
    wfull[x, y, c, 24:32, :] = wd_s[x] + wd_x[0] + wd_x[1] + wd_x[2]
    second = gather_start(wfull)
    x_wait()
    o_up = dot(p_up, xinv[0], 1, 1)
    o_down = dot(p_down, xinv[1], 1, 1)
    gather_end(wfull, *second)

    right_up = dot(wfull[:, :, :, 0:24, :].reshape(1536, RANK), xinv[0], 1, 1)
    right_down = dot(dot(pick, wfull[:, :, :, 24:32, :].reshape(512, RANK)), xinv[1], 1, 1)
    ssum[...] = jnp.zeros((8, RANK), F32)
    ssum[0:1, :] = jnp.sum(right_up * right_up, axis=0, keepdims=True)
    ssum[1:2, :] = jnp.sum(right_down * right_down, axis=0, keepdims=True)
    s_wait = [
        transfer(ssum, ssum_in.at[d - 1], along_z(d), ssum_in.at[d - 1]) for d in range(1, NZ)
    ]
    new_up[...] = blend_up[...] - (1.0 - retain) * dot(o_up, right_up, 1, 1)
    new_down[...] = blend_down[...] - (1.0 - retain) * dot(o_down, right_down, 1, 1)
    wait(s_wait)
    sums = ssum[...]
    for d in range(1, NZ):
        sums = sums + ssum_in[d - 1]
    scale = lax.rsqrt(sums + epsilon)
    s_up, s_down = scale[0:1], scale[1:2]
    upd_up[...] = math.sqrt(3072 / 12288) * dot(o_up * s_up, right_up, 1, 1)
    upd_down[...] = math.sqrt(12288 / 3072) * dot(o_down * s_down, right_down, 1, 1)
    nb_up[0] = dot(wfull[x, y, c, 0:24, :], xinv[0], 1, 1) * s_up
    nb_down[0] = (dot(wfull[x, y, c, 24:32, :], xinv[1], 1, 1) * s_down)[0:6]
    for copy in started:
        copy.wait_send()


SCRATCH = (
    [(NX, NY, 2, 32, RANK), (48, 1536), (192, 384), (192, 512)]
    + [(NZ, 32, RANK), (NZ - 1, 32, RANK), (NZ, 32, RANK)]
    + [(2, RANK, RANK), (RANK, RANK), (NX, 64, RANK), (NX - 1, 64, RANK), (NY, 8, RANK)]
    + [(NY - 1, 8, RANK), (NX, NY, 8, RANK)]
    + [(NX, NY, 2, 32, RANK), (NX, NY, 32, RANK), (NX, NY, 32, RANK)]
    + [(NX - 1, NY, 24, RANK), (NY, 24, RANK), (NY - 1, 24, RANK)]
    + [(NY - 1, NX, 8, RANK), (NX, 8, RANK), (NX - 1, 8, RANK), (NX, NY, 2, 32, RANK)]
    + [(2, RANK, RANK), (8, RANK), (NZ - 1, 8, RANK)]
)
COPIES = 128


def body(*args):
    vmem = pl.BlockSpec(memory_space=pltpu.VMEM)
    shapes = [(48, 1536), (48, 1536), (1, 24, RANK), (192, 384), (192, 384), (1, 6, RANK)]
    return pl.pallas_call(
        kernel,
        out_shape=[jax.ShapeDtypeStruct(s, F32) for s in shapes],
        in_specs=[vmem] * 6,
        out_specs=[vmem] * 6,
        scratch_shapes=[pltpu.VMEM(s, F32) for s in SCRATCH]
        + [pltpu.SemaphoreType.DMA((COPIES,))] * 2,
        compiler_params=pltpu.CompilerParams(
            collective_id=0, has_side_effects=True, vmem_limit_bytes=56 << 20
        ),
    )(*args)


def solution(mesh):
    specs = (P("fsdp", "tp"), P("fsdp", "tp"), P("tp", "fsdp", None)) * 2
    return jax.shard_map(
        body,
        mesh=mesh,
        in_specs=specs,
        out_specs=specs,
        check_vma=False,
    )
```

time: 735 us -> 132 us (0.18); the launches traced: 726 us -> 132 us
  waiting for transfers between devices: 472 us -> 0 us
  Pallas kernels: 0 us -> 124 us
  other arithmetic: 112 us -> 0 us
  blocking collectives: 89.2 us -> 0 us
  matrix products: 22.5 us -> 0 us
  between operations: 18.8 us -> 0.66 us
    psum x3 -> x0, waiting for transfers between devices: 462 us -> none  [the longest x1 197 us: body(): right = lax.psum(right_term, 'fsdp')]
    pallas_call x0 -> x1, Pallas kernels: none -> 124 us  [body(): pl.pallas_call(kernel, out_shape=[jax.ShapeDtypeStruct(s, F32) for s in s...]
    another operation x19 -> x0, other arithmetic: 109 us -> none  [the longest x14 69.2 us: body(): lower = jnp.linalg.cholesky(grams[which])]
    all_gather x1 -> x0, blocking collectives: 50.8 us -> none  [gathered(): return lax.all_gather(part, axis, axis=dim, tiled=True)]
    psum x2 -> x0, blocking collectives: 38.4 us -> none  [the longest x1 24.1 us: body(): projected = [lax.psum(term, 'tp') for term in partials]]
    dot_general x10 -> x0, matrix products: 20.3 us -> none  [the longest x4 8.07 us: outer_rows(): lax.dot_general(left, right_side, (((1,), (1,)), ((), ())), precision=HIG...]
    all_gather x1 -> x0, waiting for transfers between devices: 9.52 us -> none  [gathered(): return lax.all_gather(part, axis, axis=dim, tiled=True)]
    another operation x17 -> x0, local copies, waits for them, and re-layouts: 8.02 us -> none
  transfers between devices with their start and end apart: 4 -> 0, of which waited for: 4 -> 0; matrix products, arithmetic and copies ran while one was open for 0% -> 0% of each run, Pallas kernels for 0% -> 0%
where the time goes in v1:
time: 132 us
  Pallas kernels  124 us (94%)
  local copies, waits for them, and re-layouts  7.45 us (6%)
    pallas_call x1, Pallas kernels, body(): pl.pallas_call(kernel, out_shape=[jax.ShapeDtypeStruct(s, F32) for s in s...  124 us
    unnamed x16, local copies, waits for them, and re-layouts  6.85 us

profile of v1, /device:TPU:1, one launch (start us, length us, event | category | flops | bytes accessed | tf_op | source)
XLA Modules:
  0.0 131.6 jit_solution(13958756804719347910)
XLA Ops:
  0.6 1.3 copy.12.basis_down
  1.9 123.5 %shard_map.109 = (f32[48,1536]{1,0:T(8,128)}, f32[48,1536]{1,0:T(8,128)}, f32[1,24,256]{2,1,0:T(8,128)}, f32[192,384]{1,0:T(8,128)}, f32[192,384]{1,0:T(8,128)}, /*index=5*/f32[1,6,256]{2,1,0:T(8,128)}) custom-call(f32[48,1536]{1,0:T(8,128)} %mom_up.1, bf16[48,1536]{1,0:T(8,128)(2,1)} %grad_up.1, f32[1,24,256]{2,1,0:T(8,128)} %basis_up.1, ...), custom_call_target="tpu_custom_call" | custom-call | tf_op jit(solution)/shard_map/pallas_call | solution.py:318
  125.4 0.0 copy-start.4
  125.5 0.7 copy-done.4
  126.1 0.6 copy.13
  126.7 0.0 copy-start.2
  126.7 1.7 %copy.19 = f32[48,1536]{1,0:T(8,128)} copy(f32[48,1536]{1,0:T(8,128)} %get-tuple-element.18) | data formatting | bytes 589824
  128.5 0.0 copy-done.2
  128.5 0.0 copy-start.3
  128.5 0.0 copy-start.1
  128.5 0.7 copy.20
  129.2 0.0 copy-done.3
  129.2 0.6 copy.21
  129.8 0.0 copy-done.1
  129.8 0.0 copy-start
  129.8 0.7 copy.22
  130.6 0.4 copy-done
  130.9 0.7 copy.23
Async XLA Ops:
  125.4 0.7 copy-start.4
  126.7 1.7 %copy-start.2 = (f32[48,1536]{1,0:T(8,128)S(1)}, f32[48,1536]{1,0:T(8,128)}, u32[]{:S(2)}) copy-start(f32[48,1536]{1,0:T(8,128)} %get-tuple-element.19) | copy-start | bytes 884740
  128.5 0.7 copy-start.3
  128.5 1.3 %copy-start.1 = (f32[192,384]{1,0:T(8,128)S(1)}, f32[192,384]{1,0:T(8,128)}, u32[]{:S(2)}) copy-start(f32[192,384]{1,0:T(8,128)} %get-tuple-element.21) | copy-start | bytes 884740
  129.8 1.1 copy-start

commit v2 on v1

v2 whole, which is shorter than its diff:
```python
import math

import jax
import jax.numpy as jnp
from jax import lax
from jax.experimental import pallas as pl
from jax.experimental.pallas import tpu as pltpu
from jax.sharding import PartitionSpec as P

retain = 0.9
epsilon = 1e-06
HIGH = lax.Precision.HIGHEST
MESH = pl.DeviceIdType.MESH
NX, NY, NZ, RANK = 4, 8, 8, 256
F32 = jnp.float32


def dot(a, b, ca=1, cb=0):
    return lax.dot_general(
        a, b, (((ca,), (cb,)), ((), ())), precision=HIGH, preferred_element_type=F32
    )


def halves(v):
    high = v.astype(jnp.bfloat16)
    return high, (v - high.astype(F32)).astype(jnp.bfloat16)


def dot_halves(a, b, ca=1, cb=0):
    dims = (((ca,), (cb,)), ((), ()))

    def one(u, v):
        return lax.dot_general(u, v, dims, preferred_element_type=F32)

    return one(a[0], b[0]) + (one(a[0], b[1]) + one(a[1], b[0]))


def invert_half(a, hook=None):
    lanes = lax.broadcasted_iota(jnp.int32, (8, 128), 1)
    subs = lax.broadcasted_iota(jnp.int32, (8, 128), 0)
    groups = [a[8 * g : 8 * g + 8] for g in range(16)]
    done = []
    for k in range(16):
        base = 8 * k
        inside = (lanes >= base) & (lanes < base + 8)
        panel = groups[0]
        cols = [jnp.broadcast_to(panel[:, base + j : base + j + 1], (8, 128)) for j in range(8)]
        held = jnp.where(inside, (lanes == subs + base).astype(F32), panel)
        pivots = cols[0]
        inverse, heads = [], []
        for j in range(8):
            r = 1.0 / cols[j][j : j + 1]
            inverse.append(r)
            mult = jnp.where(subs > j, cols[j] * r, 0.0)
            heads.append([c[j : j + 1] for c in cols])
            for jj in range(j + 1, 8):
                cols[jj] = cols[jj] - mult * heads[j][jj]
            held = held - mult * held[j : j + 1]
            if j:
                pivots = jnp.where(subs == j, cols[j], pivots)
        done.append(jnp.where(lanes <= subs + base, held * lax.rsqrt(pivots), 0.0))
        rest = []
        for g in groups[1:]:
            c = [jnp.broadcast_to(g[:, base + j : base + j + 1], (8, 128)) for j in range(8)]
            out = jnp.where(inside, 0.0, g)
            for j in range(8):
                m = c[j] * inverse[j]
                for jj in range(j + 1, 8):
                    c[jj] = c[jj] - m * heads[j][jj]
                out = out - m * held[j : j + 1]
            rest.append(out)
        groups = rest
        if hook is not None:
            hook(k)
    return jnp.concatenate(done, axis=0)


def place():
    f = lax.axis_index("fsdp")
    return f // 16, lax.rem(f // 2, 8), lax.rem(f, 2), lax.axis_index("tp")


NEAR_FIRST = (1, 7, 2, 6, 3, 5, 4)
FAR_FIRST = (4, 3, 5, 2, 6, 1, 7)


def kernel(
    mom_up, grad_up, basis_up, mom_down, grad_down, basis_down,
    upd_up, new_up, nb_up, upd_down, new_down, nb_down,
    q, wfull, wpart, wcore, wsum, wu_x, wu_s, wu_y, wd_y, wd_s, wd_x,
    m_up, m_down, blend_up, blend_down, r_up, o_upd_up, o_new_up, o_upd_down, o_new_down,
    part_up, part_up_in, pfull_up, part_down, part_down_in, pfull_down,
    gram, gram_in, gsum, g_x, g_xs, g_y, g_all, xinv, ssum, ssum_in,
    g_up, g_down, bu_hi, bu_lo, pd_hi, pd_lo, tu_hi, tu_lo, td_hi, td_lo,
    send, recv, local,
):
    x, y, c, z = place()
    count = [0]

    def at(xx, yy, cc, zz):
        return (xx * 16 + yy * 2 + cc, zz)

    def along_y(d):
        return at(x, lax.rem(y + d, NY), c, z)

    def along_x(d):
        return at(lax.rem(x + d, NX), y, c, z)

    def along_z(d):
        return at(x, y, c, lax.rem(z + d, NZ))

    sibling = at(x, y, 1 - c, z)

    barrier = pltpu.get_barrier_semaphore()
    peers = (
        [along_y(d) for d in range(1, NY)]
        + [along_x(d) for d in range(1, NX)]
        + [along_z(d) for d in range(1, NZ)]
        + [sibling]
    )
    for peer in peers:
        pl.semaphore_signal(barrier, inc=1, device_id=peer, device_id_type=MESH)
    loads = [
        pltpu.make_async_copy(src, dst, local.at[i])
        for i, (src, dst) in enumerate(
            ((mom_down, m_down), (grad_down, g_down), (mom_up, m_up), (grad_up, g_up))
        )
    ]
    for load in loads:
        load.start()

    started = []

    def transfer(src, dst, device, arrives):
        n = count[0]
        count[0] += 1
        copy = pltpu.make_async_remote_copy(
            src, dst, send.at[n], recv.at[n], device_id=device, device_id_type=MESH
        )
        copy.start()
        started.append(copy)
        landing = pltpu.make_async_remote_copy(
            src, arrives, send.at[n], recv.at[n], device_id=device, device_id_type=MESH
        )
        return landing.wait_recv

    def wait(waits):
        for w in waits:
            w()

    def back(v, d, n):
        return lax.rem(v + n - d, n)

    class Gather:
        def __init__(self, buf):
            self.buf = buf
            self.down_x = [
                transfer(buf.at[x, y, c, 24:32], buf.at[x, y, c, 24:32], along_x(d),
                         buf.at[back(x, d, NX), y, c, 24:32])
                for d in range(1, NX)
            ]
            self.up_y = {
                d: transfer(buf.at[x, y, c, 0:24], buf.at[x, y, c, 0:24], along_y(d),
                            buf.at[x, back(y, d, NY), c, 0:24])
                for d in NEAR_FIRST
            }
            self.up_x = {d: [] for d in range(1, NX)}
            self.forward(y)

        def forward(self, yy):
            for d in range(1, NX):
                piece = self.buf.at[x, yy, c, 0:24]
                self.up_x[d].append(
                    transfer(piece, piece, along_x(d), self.buf.at[back(x, d, NX), yy, c, 0:24])
                )

        def second(self):
            buf = self.buf
            wait(self.down_x)
            self.down_y = [
                transfer(buf.at[:, y, c, 24:32], buf.at[:, y, c, 24:32], along_y(d),
                         buf.at[:, back(y, d, NY), c, 24:32])
                for d in range(1, NY)
            ]
            for d in NEAR_FIRST:
                self.up_y[d]()
                self.forward(back(y, d, NY))
            self.cores = [self.across(x)]

        def across(self, xx):
            block = self.buf.at[xx, :, c, 0:24]
            return transfer(block, block, sibling, self.buf.at[xx, :, 1 - c, 0:24])

        def down(self):
            wait(self.down_y)
            block = self.buf.at[:, :, c, 24:32]
            transfer(block, block, sibling, self.buf.at[:, :, 1 - c, 24:32])()

        def up(self, use):
            for d in range(1, NX):
                wait(self.up_x[d])
                self.cores.append(self.across(back(x, d, NX)))
                self.cores[d - 1]()
                use(back(x, d - 1, NX))
            self.cores[NX - 1]()
            use(back(x, NX - 1, NX))

    q[x, y, c, 0:24, :] = basis_up[0]
    q[x, y, c, 24:32, :] = jnp.zeros((8, RANK), F32)
    for i in range(6):
        q[x, y, c, 24 + i : 25 + i, :] = basis_down[i]
    pl.semaphore_wait(barrier, len(peers))
    first = Gather(q)

    column = lax.broadcasted_iota(jnp.int32, (384, 512), 0)
    slot = lax.broadcasted_iota(jnp.int32, (384, 512), 1)
    pick = ((column == (slot // 8) * 6 + lax.rem(slot, 8)) & (lax.rem(slot, 8) < 6)).astype(F32)
    for load in loads:
        load.wait()
    blend_down[...] = m_down[...] + g_down[...].astype(F32)
    blend_up[...] = m_up[...] + g_up[...].astype(F32)
    for g in range(NX):
        bu_hi[g], bu_lo[g] = halves(blend_up[:, 384 * g : 384 * g + 384])
    padded = dot(blend_down[...], pick)
    pd_hi[...], pd_lo[...] = halves(padded)
    first.second()
    first.down()

    p_part = dot_halves(
        (pd_hi[...], pd_lo[...]), halves(q[:, :, :, 24:32, :].reshape(512, RANK))
    )
    part_down[...] = p_part.reshape(NZ, 24, RANK)

    def reduce_z(part, part_in):
        return [
            transfer(part.at[lax.rem(z + d, NZ)], part_in.at[d - 1], along_z(d), part_in.at[d - 1])
            for d in FAR_FIRST
        ]

    def gather_z(part, part_in, full):
        total = part[z]
        for d in range(1, NZ):
            total = total + part_in[d - 1]
        full[z] = total
        return [
            transfer(full.at[z], full.at[z], along_z(d), full.at[back(z, d, NZ)])
            for d in FAR_FIRST
        ]

    down_rs = reduce_z(part_down, part_down_in)
    sums_up = []

    def add_up(g):
        piece = halves(q[g, :, :, 0:24, :].reshape(384, RANK))
        sums_up.append(dot_halves((bu_hi[g], bu_lo[g]), piece))

    first.up(add_up)
    part_up[0:6] = (sums_up[0] + sums_up[1] + sums_up[2] + sums_up[3]).reshape(6, 8, RANK)
    part_up[6:8] = jnp.zeros((2, 8, RANK), F32)
    up_rs = reduce_z(part_up, part_up_in)
    for g in range(NX):
        tu_hi[g], tu_lo[g] = halves(blend_up[:, 384 * g : 384 * g + 384].T)
    td_hi[...], td_lo[...] = halves(padded.T)
    wait(down_rs)
    down_ag = gather_z(part_down, part_down_in, pfull_down)
    wait(up_rs)
    up_ag = gather_z(part_up, part_up_in, pfull_up)

    wait(down_ag)
    p_down = pfull_down[...].reshape(192, RANK)
    gram[1] = dot(p_down, p_down, 0, 0)
    wait(up_ag)
    p_up = pfull_up[0:6].reshape(48, RANK)
    gram[0] = dot(p_up, p_up, 0, 0)
    gram_wait = transfer(gram.at[1 - c], gram_in, sibling, gram_in)
    gram_wait()
    gsum[...] = (gram[c] + gram_in[...]).reshape(NX, 64, RANK)
    gram_x = [
        transfer(gsum.at[lax.rem(x + d, NX)], g_x.at[d - 1], along_x(d), g_x.at[d - 1])
        for d in (2, 1, 3)
    ]
    p_halves = halves(p_down)
    wpart[:, :, :, 24:32, :] = dot_halves((td_hi[...], td_lo[...]), p_halves).reshape(
        NX, NY, 2, 8, RANK
    )
    core_down = transfer(
        wpart.at[:, :, 1 - c, 24:32], wcore.at[:, :, 24:32], sibling, wcore.at[:, :, 24:32]
    )
    p_halves = halves(p_up)
    for g in range(NX):
        wpart[g, :, :, 0:24, :] = dot_halves((tu_hi[g], tu_lo[g]), p_halves).reshape(
            NY, 2, 24, RANK
        )
    core_up = transfer(
        wpart.at[:, :, 1 - c, 0:24], wcore.at[:, :, 0:24], sibling, wcore.at[:, :, 0:24]
    )
    wait(gram_x)
    g_xs[...] = (gsum[x] + g_x[0] + g_x[1] + g_x[2]).reshape(NY, 8, RANK)
    gram_y = [
        transfer(g_xs.at[lax.rem(y + d, NY)], g_y.at[d - 1], along_y(d), g_y.at[d - 1])
        for d in FAR_FIRST
    ]
    core_down()
    core_up()
    wsum[...] = wpart[:, :, c] + wcore[...]
    w_x = {}

    def scatter_x(d):
        yy = lax.rem(y + d, NY)
        w_x[d] = [
            transfer(wsum.at[lax.rem(x + e, NX), yy, 0:24], wu_x.at[e - 1, d], along_x(e),
                     wu_x.at[e - 1, d])
            for e in (2, 1, 3)
        ]

    w_y = []

    def scatter_y(d):
        wait(w_x[d])
        wu_s[d] = wsum[x, lax.rem(y + d, NY), 0:24] + wu_x[0, d] + wu_x[1, d] + wu_x[2, d]
        if d:
            w_y.append(transfer(wu_s.at[d], wu_y.at[d - 1], along_y(d), wu_y.at[d - 1]))

    for d in (4, 3, 5, 2):
        scatter_x(d)
    wait(gram_y)
    row = g_xs[y]
    for d in range(1, NY):
        row = row + g_y[d - 1]
    g_all[x, y] = row
    gram_y = [
        transfer(g_all.at[x, y], g_all.at[x, y], along_y(d), g_all.at[x, back(y, d, NY)])
        for d in FAR_FIRST
    ]
    down_y = [
        transfer(wsum.at[:, lax.rem(y + d, NY), 24:32], wd_y.at[d - 1], along_y(d), wd_y.at[d - 1])
        for d in FAR_FIRST
    ]
    wait(gram_y)
    gram_x = [
        transfer(g_all.at[x], g_all.at[x], along_x(d), g_all.at[back(x, d, NX)])
        for d in (2, 1, 3)
    ]
    for d in (6, 1, 7, 0):
        scatter_x(d)
    for d in (4, 3, 5, 2):
        scatter_y(d)
    wait(gram_x)

    g11, g12, g22 = (
        g_all[0:2, :, :, 0:128].reshape(128, 128),
        g_all[0:2, :, :, 128:256].reshape(128, 128),
        g_all[2:4, :, :, 128:256].reshape(128, 128),
    )
    down_x = []

    def scatter_down():
        wait(down_y)
        owned = wsum[:, y, 24:32]
        for d in range(1, NY):
            owned = owned + wd_y[d - 1]
        wd_s[...] = owned
        down_x.extend(
            transfer(wd_s.at[lax.rem(x + d, NX)], wd_x.at[d - 1], along_x(d), wd_x.at[d - 1])
            for d in (2, 1, 3)
        )

    def hook(k):
        if k == 3:
            scatter_y(6)
        if k == 5:
            scatter_down()
        if k == 7:
            scatter_y(1)
            scatter_y(7)
        if k == 9:
            scatter_y(0)

    x11 = invert_half(g11, hook)
    xinv[c, 0:128, 0:128] = x11
    xinv[c, 0:128, 128:256] = jnp.zeros((128, 128), F32)
    u = dot(x11, g12)
    low = g22 - dot(u, u, 0, 0)
    corner = dot(u, x11, 0, 0)
    gathers = []

    def hook(k):
        if k == 5:
            wait(w_y)
            owned = wu_s[0]
            for d in range(1, NY):
                owned = owned + wu_y[d - 1]
            wfull[x, y, c, 0:24, :] = owned
            wait(down_x)
            wfull[x, y, c, 24:32, :] = wd_s[x] + wd_x[0] + wd_x[1] + wd_x[2]
            gathers.append(Gather(wfull))
        if k == 13:
            gathers[0].second()

    x22 = invert_half(low, hook)
    xinv[c, 128:256, 128:256] = x22
    xinv[c, 128:256, 0:128] = -dot(x22, corner)
    x_wait = transfer(xinv.at[c], xinv.at[c], sibling, xinv.at[1 - c])
    x_wait()
    o_up = dot(p_up, xinv[0], 1, 1)
    o_down = dot(p_down, xinv[1], 1, 1)
    x_up, x_down = halves(xinv[0]), halves(xinv[1])
    ou_halves, od_halves = halves(o_up), halves(o_down)

    last = gathers[0]
    last.down()
    right_down = dot_halves(
        halves(dot(pick, wfull[:, :, :, 24:32, :].reshape(512, RANK))), x_down, 1, 1
    )
    rd_halves = halves(right_down)
    o_new_down[...] = blend_down[...] - (1.0 - retain) * dot_halves(od_halves, rd_halves, 1, 1)
    writes = []

    def write(src, dst):
        copy = pltpu.make_async_copy(src, dst, local.at[4 + len(writes)])
        copy.start()
        writes.append(copy)

    write(o_new_down, new_down)
    squares = []

    def turn(g):
        right = dot_halves(halves(wfull[g, :, :, 0:24, :].reshape(384, RANK)), x_up, 1, 1)
        r_up[g] = right
        squares.append(jnp.sum(right * right, axis=0, keepdims=True))

    last.up(turn)
    ssum[...] = jnp.zeros((8, RANK), F32)
    ssum[0:1, :] = squares[0] + squares[1] + squares[2] + squares[3]
    ssum[1:2, :] = jnp.sum(right_down * right_down, axis=0, keepdims=True)
    s_wait = [
        transfer(ssum, ssum_in.at[d - 1], along_z(d), ssum_in.at[d - 1]) for d in FAR_FIRST
    ]
    ru_halves = [halves(r_up[g]) for g in range(NX)]
    for g in range(NX):
        cols = slice(384 * g, 384 * g + 384)
        o_new_up[:, cols] = blend_up[:, cols] - (1.0 - retain) * dot_halves(
            ou_halves, ru_halves[g], 1, 1
        )
    write(o_new_up, new_up)
    wait(s_wait)
    sums = ssum[...]
    for d in range(1, NZ):
        sums = sums + ssum_in[d - 1]
    scale = lax.rsqrt(sums + epsilon)
    s_up, s_down = scale[0:1], scale[1:2]
    ou_halves = halves(math.sqrt(3072 / 12288) * o_up * s_up)
    for g in range(NX):
        o_upd_up[:, 384 * g : 384 * g + 384] = dot_halves(ou_halves, ru_halves[g], 1, 1)
    write(o_upd_up, upd_up)
    od_halves = halves(math.sqrt(12288 / 3072) * o_down * s_down)
    o_upd_down[...] = dot_halves(od_halves, rd_halves, 1, 1)
    write(o_upd_down, upd_down)
    nb_up[0] = dot(wfull[x, y, c, 0:24, :], xinv[0], 1, 1) * s_up
    nb = dot(wfull[x, y, c, 24:32, :], xinv[1], 1, 1) * s_down
    for i in range(6):
        nb_down[i] = nb[i : i + 1]
    for copy in started:
        copy.wait_send()
    for copy in writes:
        copy.wait()


PIECES = (NX, NY, 2, 32, RANK)
SCRATCH = (
    [PIECES, PIECES, PIECES, (NX, NY, 32, RANK), (NX, NY, 32, RANK)]
    + [(NX - 1, NY, 24, RANK), (NY, 24, RANK), (NY - 1, 24, RANK)]
    + [(NY - 1, NX, 8, RANK), (NX, 8, RANK), (NX - 1, 8, RANK)]
    + [(48, 1536), (192, 384), (48, 1536), (192, 384), (NX, 384, RANK)]
    + [(48, 1536), (48, 1536), (192, 384), (192, 384)]
    + [(NZ, 8, RANK), (NZ - 1, 8, RANK), (NZ, 8, RANK)]
    + [(NZ, 24, RANK), (NZ - 1, 24, RANK), (NZ, 24, RANK)]
    + [(2, RANK, RANK), (RANK, RANK), (NX, 64, RANK), (NX - 1, 64, RANK), (NY, 8, RANK)]
    + [(NY - 1, 8, RANK), (NX, NY, 8, RANK)]
    + [(2, RANK, RANK), (8, RANK), (NZ - 1, 8, RANK)]
)
HALF_SCRATCH = (
    [(48, 1536), (192, 384)]
    + [(NX, 48, 384)] * 2
    + [(192, 512)] * 2
    + [(NX, 384, 48)] * 2
    + [(512, 192)] * 2
)
COPIES = 224


def finish(*refs):
    sources, results, sems = refs[0:6], refs[6:12], refs[12]
    copies = [
        pltpu.make_async_copy(src, dst, sems.at[i])
        for i, (src, dst) in enumerate(zip(sources, results))
    ]
    for copy in copies:
        copy.start()
    for copy in copies:
        copy.wait()


def body(mom_up, grad_up, basis_up, mom_down, grad_down, basis_down):
    vmem = pl.BlockSpec(memory_space=pltpu.VMEM)
    anywhere = pl.BlockSpec(memory_space=pl.ANY)
    shapes = [(48, 1536), (48, 1536), (1, 24, RANK), (192, 384), (192, 384), (6, 1, RANK)]
    out_shape = [jax.ShapeDtypeStruct(s, F32) for s in shapes]
    results = pl.pallas_call(
        kernel,
        out_shape=out_shape,
        in_specs=[anywhere, anywhere, vmem] * 2,
        out_specs=[anywhere, anywhere, vmem] * 2,
        scratch_shapes=[pltpu.VMEM(s, F32) for s in SCRATCH]
        + [pltpu.VMEM(s, jnp.bfloat16) for s in HALF_SCRATCH]
        + [pltpu.SemaphoreType.DMA((COPIES,))] * 2
        + [pltpu.SemaphoreType.DMA((8,))],
        compiler_params=pltpu.CompilerParams(
            collective_id=0, has_side_effects=True, vmem_limit_bytes=60 << 20
        ),
    )(mom_up, grad_up, basis_up, mom_down, grad_down, jnp.swapaxes(basis_down, 0, 1))
    results = pl.pallas_call(
        finish,
        out_shape=out_shape,
        in_specs=[anywhere] * 6,
        out_specs=[anywhere] * 6,
        scratch_shapes=[pltpu.SemaphoreType.DMA((6,))],
    )(*results)
    return (*results[:5], jnp.swapaxes(results[5], 0, 1))


def solution(mesh):
    specs = (P("fsdp", "tp"), P("fsdp", "tp"), P("tp", "fsdp", None)) * 2
    return jax.shard_map(
        body,
        mesh=mesh,
        in_specs=specs,
        out_specs=specs,
        check_vma=False,
    )
```

time: 132 us -> 143 us (1.083)
  Pallas kernels: 124 us -> 142 us
  local copies, waits for them, and re-layouts: 7.45 us -> 0 us
    pallas_call x1 -> x2, Pallas kernels: 124 us -> 142 us  [the longest x1 104 us: body(): pl.pallas_call(kernel, out_shape=out_shape, in_specs=[anywhere, anywhere,...]
    unnamed x16 -> x0, local copies, waits for them, and re-layouts: 6.85 us -> none
where the time goes in v2:
time: 143 us
  Pallas kernels  142 us (99%)
    pallas_call x1, Pallas kernels, body(): pl.pallas_call(kernel, out_shape=out_shape, in_specs=[anywhere, anywhere,...  104 us
    pallas_call x1, Pallas kernels, body(): pl.pallas_call(finish, out_shape=out_shape, in_specs=[anywhere] * 6, out_...  37.8 us

profile of v2, /device:TPU:1, one launch (start us, length us, event | category | flops | bytes accessed | tf_op | source)
XLA Modules:
  0.0 142.9 jit_solution(16874196978064627590)
XLA Ops:
  0.6 104.3 %shard_map.109 = (f32[48,1536]{1,0:T(8,128)}, f32[48,1536]{1,0:T(8,128)}, f32[1,24,256]{2,1,0:T(8,128)}, f32[192,384]{1,0:T(8,128)}, f32[192,384]{1,0:T(8,128)}, /*index=5*/f32[6,1,256]{2,1,0:T(1,128)}) custom-call(f32[48,1536]{1,0:T(8,128)} %mom_up.1, bf16[48,1536]{1,0:T(8,128)(2,1)} %grad_up.1, f32[1,24,256]{2,1,0:T(8,128)} %basis_up.1, ...), custom_call_target="tpu_custom_call" | custom-call | tf_op jit(solution)/shard_map/pallas_call | solution.py:509
  105.0 37.8 %shard_map.110 = (f32[48,1536]{1,0:T(8,128)}, f32[48,1536]{1,0:T(8,128)}, f32[1,24,256]{2,1,0:T(8,128)}, f32[192,384]{1,0:T(8,128)}, f32[192,384]{1,0:T(8,128)}, /*index=5*/f32[6,1,256]{2,1,0:T(1,128)}) custom-call(f32[48,1536]{1,0:T(8,128)} %get-tuple-element.18.refs_0_, f32[48,1536]{1,0:T(8,128)} %get-tuple-element.19.refs_1_, ...), custom_call_target="tpu_custom_call" | custom-call | tf_op jit(solution)/shard_map/pallas_call | solution.py:522

commit v3 on v2

--- a/solution.py
+++ b/solution.py
@@ -90,7 +90,7 @@
     q, wfull, wpart, wcore, wsum, wu_x, wu_s, wu_y, wd_y, wd_s, wd_x,
     m_up, m_down, blend_up, blend_down, r_up, o_upd_up, o_new_up, o_upd_down, o_new_down,
     part_up, part_up_in, pfull_up, part_down, part_down_in, pfull_down,
-    gram, gram_in, gsum, g_x, g_xs, g_y, g_all, xinv, ssum, ssum_in,
+    gram, gram_in, gsum, g_x, g_y, g_all, xinv, ssum, ssum_in,
     g_up, g_down, bu_hi, bu_lo, pd_hi, pd_lo, tu_hi, tu_lo, td_hi, td_lo,
     send, recv, local,
 ):
@@ -168,24 +168,37 @@
             self.forward(y)
 
         def forward(self, yy):
-            for d in range(1, NX):
+            for d in (2, 1, 3):
                 piece = self.buf.at[x, yy, c, 0:24]
                 self.up_x[d].append(
                     transfer(piece, piece, along_x(d), self.buf.at[back(x, d, NX), yy, c, 0:24])
                 )
 
-        def second(self):
+        def turn(self):
             buf = self.buf
             wait(self.down_x)
             self.down_y = [
                 transfer(buf.at[:, y, c, 24:32], buf.at[:, y, c, 24:32], along_y(d),
                          buf.at[:, back(y, d, NY), c, 24:32])
-                for d in range(1, NY)
+                for d in FAR_FIRST
             ]
-            for d in NEAR_FIRST:
+
+        def relay(self, *steps):
+            for d in steps:
                 self.up_y[d]()
                 self.forward(back(y, d, NY))
-            self.cores = [self.across(x)]
+
+        def own(self):
+            self.cores = {0: self.across(x)}
+
+        def column(self, d):
+            wait(self.up_x[d])
+            self.cores[d] = self.across(back(x, d, NX))
+
+        def second(self):
+            self.turn()
+            self.relay(*NEAR_FIRST)
+            self.own()
 
         def across(self, xx):
             block = self.buf.at[xx, :, c, 0:24]
@@ -194,16 +207,18 @@
         def down(self):
             wait(self.down_y)
             block = self.buf.at[:, :, c, 24:32]
-            transfer(block, block, sibling, self.buf.at[:, :, 1 - c, 24:32])()
+            return transfer(block, block, sibling, self.buf.at[:, :, 1 - c, 24:32])
 
         def up(self, use):
-            for d in range(1, NX):
-                wait(self.up_x[d])
-                self.cores.append(self.across(back(x, d, NX)))
-                self.cores[d - 1]()
-                use(back(x, d - 1, NX))
-            self.cores[NX - 1]()
-            use(back(x, NX - 1, NX))
+            before = 0
+            for d in (1, 3, 2):
+                if d not in self.cores:
+                    self.column(d)
+                self.cores[before]()
+                use(back(x, before, NX))
+                before = d
+            self.cores[before]()
+            use(back(x, before, NX))
 
     q[x, y, c, 0:24, :] = basis_up[0]
     q[x, y, c, 24:32, :] = jnp.zeros((8, RANK), F32)
@@ -224,7 +239,7 @@
     padded = dot(blend_down[...], pick)
     pd_hi[...], pd_lo[...] = halves(padded)
     first.second()
-    first.down()
+    first.down()()
 
     p_part = dot_halves(
         (pd_hi[...], pd_lo[...]), halves(q[:, :, :, 24:32, :].reshape(512, RANK))
@@ -268,50 +283,36 @@
 
     wait(down_ag)
     p_down = pfull_down[...].reshape(192, RANK)
-    gram[1] = dot(p_down, p_down, 0, 0)
+    gram[1] = dot(p_down, p_down, 0, 0).reshape(NZ, 32, RANK)
     wait(up_ag)
     p_up = pfull_up[0:6].reshape(48, RANK)
-    gram[0] = dot(p_up, p_up, 0, 0)
-    gram_wait = transfer(gram.at[1 - c], gram_in, sibling, gram_in)
-    gram_wait()
-    gsum[...] = (gram[c] + gram_in[...]).reshape(NX, 64, RANK)
-    gram_x = [
-        transfer(gsum.at[lax.rem(x + d, NX)], g_x.at[d - 1], along_x(d), g_x.at[d - 1])
-        for d in (2, 1, 3)
-    ]
-    p_halves = halves(p_down)
-    wpart[:, :, :, 24:32, :] = dot_halves((td_hi[...], td_lo[...]), p_halves).reshape(
-        NX, NY, 2, 8, RANK
-    )
-    core_down = transfer(
-        wpart.at[:, :, 1 - c, 24:32], wcore.at[:, :, 24:32], sibling, wcore.at[:, :, 24:32]
-    )
+    gram[0] = dot(p_up, p_up, 0, 0).reshape(NZ, 32, RANK)
+    gram_wait = transfer(gram.at[1 - c, z], gram_in, sibling, gram_in)
     p_halves = halves(p_up)
-    for g in range(NX):
+    core_up = {}
+
+    def multiply(e):
+        g = lax.rem(x + e, NX)
         wpart[g, :, :, 0:24, :] = dot_halves((tu_hi[g], tu_lo[g]), p_halves).reshape(
             NY, 2, 24, RANK
         )
-    core_up = transfer(
-        wpart.at[:, :, 1 - c, 0:24], wcore.at[:, :, 0:24], sibling, wcore.at[:, :, 0:24]
-    )
-    wait(gram_x)
-    g_xs[...] = (gsum[x] + g_x[0] + g_x[1] + g_x[2]).reshape(NY, 8, RANK)
-    gram_y = [
-        transfer(g_xs.at[lax.rem(y + d, NY)], g_y.at[d - 1], along_y(d), g_y.at[d - 1])
-        for d in FAR_FIRST
-    ]
-    core_down()
-    core_up()
-    wsum[...] = wpart[:, :, c] + wcore[...]
-    w_x = {}
-
-    def scatter_x(d):
+        core_up[e] = transfer(
+            wpart.at[g, :, 1 - c, 0:24], wcore.at[g, :, 0:24], sibling, wcore.at[g, :, 0:24]
+        )
+
+    def join(e):
+        g = lax.rem(x + e, NX)
+        core_up[e]()
+        wsum[g, :, 0:24] = wpart[g, :, c, 0:24] + wcore[g, :, 0:24]
+
+    w_x = {d: [] for d in range(NY)}
+
+    def scatter_x(e, d):
         yy = lax.rem(y + d, NY)
-        w_x[d] = [
+        w_x[d].append(
             transfer(wsum.at[lax.rem(x + e, NX), yy, 0:24], wu_x.at[e - 1, d], along_x(e),
                      wu_x.at[e - 1, d])
-            for e in (2, 1, 3)
-        ]
+        )
 
     w_y = []
 
@@ -321,60 +322,101 @@
         if d:
             w_y.append(transfer(wu_s.at[d], wu_y.at[d - 1], along_y(d), wu_y.at[d - 1]))
 
-    for d in (4, 3, 5, 2):
-        scatter_x(d)
-    wait(gram_y)
-    row = g_xs[y]
-    for d in range(1, NY):
-        row = row + g_y[d - 1]
-    g_all[x, y] = row
+    multiply(2)
+    gram_wait()
+    gsum[...] = (gram[c, z] + gram_in[...]).reshape(NX, 8, RANK)
+    gram_x = [
+        transfer(gsum.at[lax.rem(x + d, NX)], g_x.at[d - 1], along_x(d), g_x.at[d - 1])
+        for d in (2, 1, 3)
+    ]
+    multiply(1)
+    multiply(3)
+    join(2)
+    for d in FAR_FIRST + (0,):
+        scatter_x(2, d)
+    wait(gram_x)
+    g_y[y] = gsum[x] + g_x[0] + g_x[1] + g_x[2]
     gram_y = [
-        transfer(g_all.at[x, y], g_all.at[x, y], along_y(d), g_all.at[x, back(y, d, NY)])
-        for d in FAR_FIRST
-    ]
+        transfer(g_y.at[y], g_y.at[y], along_y(d), g_y.at[back(y, d, NY)]) for d in FAR_FIRST
+    ]
+    wpart[:, :, :, 24:32, :] = dot_halves((td_hi[...], td_lo[...]), halves(p_down)).reshape(
+        NX, NY, 2, 8, RANK
+    )
+    core_down = transfer(
+        wpart.at[:, :, 1 - c, 24:32], wcore.at[:, :, 24:32], sibling, wcore.at[:, :, 24:32]
+    )
+    join(1)
+    join(3)
+    for d in FAR_FIRST + (0,):
+        scatter_x(1, d)
+        scatter_x(3, d)
+    multiply(0)
+    core_down()
+    wsum[:, :, 24:32] = wpart[:, :, c, 24:32] + wcore[:, :, 24:32]
     down_y = [
         transfer(wsum.at[:, lax.rem(y + d, NY), 24:32], wd_y.at[d - 1], along_y(d), wd_y.at[d - 1])
         for d in FAR_FIRST
     ]
+    join(0)
     wait(gram_y)
-    gram_x = [
-        transfer(g_all.at[x], g_all.at[x], along_x(d), g_all.at[back(x, d, NX)])
+    row = g_y[0]
+    for i in range(1, NY):
+        row = row + g_y[i]
+    g_all[z, x] = row
+    gram_z = [
+        transfer(g_all.at[z, x], g_all.at[z, x], along_z(d), g_all.at[back(z, d, NZ), x])
+        for d in FAR_FIRST
+    ]
+    for d in FAR_FIRST[:3]:
+        scatter_y(d)
+    wait(gram_z)
+    gram_x = []
+    for d in (2, 1, 3):
+        xx = back(x, d, NX)
+        gram_x.append(transfer(g_all.at[0:4, x], g_all.at[0:4, x], along_x(d), g_all.at[0:4, xx]))
+        gram_x.append(
+            transfer(g_all.at[4:8, x, :, 128:256], g_all.at[4:8, x, :, 128:256], along_x(d),
+                     g_all.at[4:8, xx, :, 128:256])
+        )
+    for d in FAR_FIRST[3:]:
+        scatter_y(d)
+    wait(down_y)
+    owned = wsum[:, y, 24:32]
+    for d in range(1, NY):
+        owned = owned + wd_y[d - 1]
+    wd_s[...] = owned
+    down_x = [
+        transfer(wd_s.at[lax.rem(x + d, NX)], wd_x.at[d - 1], along_x(d), wd_x.at[d - 1])
         for d in (2, 1, 3)
     ]
-    for d in (6, 1, 7, 0):
-        scatter_x(d)
-    for d in (4, 3, 5, 2):
-        scatter_y(d)
+    scatter_y(0)
+    wait(w_y)
+    owned = wu_s[0]
+    for d in range(1, NY):
+        owned = owned + wu_y[d - 1]
+    wfull[x, y, c, 0:24, :] = owned
+    wait(down_x)
+    wfull[x, y, c, 24:32, :] = wd_s[x] + wd_x[0] + wd_x[1] + wd_x[2]
+    last = Gather(wfull)
     wait(gram_x)
 
     g11, g12, g22 = (
-        g_all[0:2, :, :, 0:128].reshape(128, 128),
-        g_all[0:2, :, :, 128:256].reshape(128, 128),
-        g_all[2:4, :, :, 128:256].reshape(128, 128),
-    )
-    down_x = []
-
-    def scatter_down():
-        wait(down_y)
-        owned = wsum[:, y, 24:32]
-        for d in range(1, NY):
-            owned = owned + wd_y[d - 1]
-        wd_s[...] = owned
-        down_x.extend(
-            transfer(wd_s.at[lax.rem(x + d, NX)], wd_x.at[d - 1], along_x(d), wd_x.at[d - 1])
-            for d in (2, 1, 3)
-        )
+        g_all[0:4, :, :, 0:128].reshape(128, 128),
+        g_all[0:4, :, :, 128:256].reshape(128, 128),
+        g_all[4:8, :, :, 128:256].reshape(128, 128),
+    )
 
     def hook(k):
-        if k == 3:
-            scatter_y(6)
+        if k == 1:
+            last.relay(1, 7)
+            last.turn()
         if k == 5:
-            scatter_down()
-        if k == 7:
-            scatter_y(1)
-            scatter_y(7)
+            last.relay(2, 6)
         if k == 9:
-            scatter_y(0)
+            last.relay(3, 5)
+        if k == 12:
+            last.relay(4)
+            last.own()
 
     x11 = invert_half(g11, hook)
     xinv[c, 0:128, 0:128] = x11
@@ -382,46 +424,28 @@
     u = dot(x11, g12)
     low = g22 - dot(u, u, 0, 0)
     corner = dot(u, x11, 0, 0)
-    gathers = []
+
+    late = []
 
     def hook(k):
-        if k == 5:
-            wait(w_y)
-            owned = wu_s[0]
-            for d in range(1, NY):
-                owned = owned + wu_y[d - 1]
-            wfull[x, y, c, 0:24, :] = owned
-            wait(down_x)
-            wfull[x, y, c, 24:32, :] = wd_s[x] + wd_x[0] + wd_x[1] + wd_x[2]
-            gathers.append(Gather(wfull))
-        if k == 13:
-            gathers[0].second()
+        if k == 6:
+            late.append(last.down())
+        if k == 9:
+            last.column(1)
+        if k == 11:
+            late[0]()
+            late.append(halves(dot(pick, wfull[:, :, :, 24:32, :].reshape(512, RANK))))
+        if k == 12:
+            last.column(3)
 
     x22 = invert_half(low, hook)
     xinv[c, 128:256, 128:256] = x22
     xinv[c, 128:256, 0:128] = -dot(x22, corner)
     x_wait = transfer(xinv.at[c], xinv.at[c], sibling, xinv.at[1 - c])
     x_wait()
-    o_up = dot(p_up, xinv[0], 1, 1)
-    o_down = dot(p_down, xinv[1], 1, 1)
     x_up, x_down = halves(xinv[0]), halves(xinv[1])
-    ou_halves, od_halves = halves(o_up), halves(o_down)
-
-    last = gathers[0]
-    last.down()
-    right_down = dot_halves(
-        halves(dot(pick, wfull[:, :, :, 24:32, :].reshape(512, RANK))), x_down, 1, 1
-    )
-    rd_halves = halves(right_down)
-    o_new_down[...] = blend_down[...] - (1.0 - retain) * dot_halves(od_halves, rd_halves, 1, 1)
-    writes = []
-
-    def write(src, dst):
-        copy = pltpu.make_async_copy(src, dst, local.at[4 + len(writes)])
-        copy.start()
-        writes.append(copy)
-
-    write(o_new_down, new_down)
+
+    right_down = dot_halves(late[1], x_down, 1, 1)
     squares = []
 
     def turn(g):
@@ -436,6 +460,19 @@
     s_wait = [
         transfer(ssum, ssum_in.at[d - 1], along_z(d), ssum_in.at[d - 1]) for d in FAR_FIRST
     ]
+    o_up = dot_halves(halves(p_up), x_up, 1, 1)
+    o_down = dot_halves(halves(p_down), x_down, 1, 1)
+    ou_halves, od_halves = halves(o_up), halves(o_down)
+    rd_halves = halves(right_down)
+    writes = []
+
+    def write(src, dst):
+        copy = pltpu.make_async_copy(src, dst, local.at[4 + len(writes)])
+        copy.start()
+        writes.append(copy)
+
+    o_new_down[...] = blend_down[...] - (1.0 - retain) * dot_halves(od_halves, rd_halves, 1, 1)
+    write(o_new_down, new_down)
     ru_halves = [halves(r_up[g]) for g in range(NX)]
     for g in range(NX):
         cols = slice(384 * g, 384 * g + 384)
@@ -443,6 +480,9 @@
             ou_halves, ru_halves[g], 1, 1
         )
     write(o_new_up, new_up)
+    nb = dot_halves(halves(wfull[x, y, c, 24:32, :]), x_down, 1, 1)
+    while started:
+        started.pop().wait_send()
     wait(s_wait)
     sums = ssum[...]
     for d in range(1, NZ):
@@ -456,12 +496,10 @@
     od_halves = halves(math.sqrt(12288 / 3072) * o_down * s_down)
     o_upd_down[...] = dot_halves(od_halves, rd_halves, 1, 1)
     write(o_upd_down, upd_down)
-    nb_up[0] = dot(wfull[x, y, c, 0:24, :], xinv[0], 1, 1) * s_up
-    nb = dot(wfull[x, y, c, 24:32, :], xinv[1], 1, 1) * s_down
+    nb_up[0] = r_up[x, pl.ds(pl.multiple_of(48 * y + 24 * c, 8), 24), :] * s_up
+    nb = nb * s_down
     for i in range(6):
         nb_down[i] = nb[i : i + 1]
-    for copy in started:
-        copy.wait_send()
     for copy in writes:
         copy.wait()
 
@@ -475,8 +513,8 @@
     + [(48, 1536), (48, 1536), (192, 384), (192, 384)]
     + [(NZ, 8, RANK), (NZ - 1, 8, RANK), (NZ, 8, RANK)]
     + [(NZ, 24, RANK), (NZ - 1, 24, RANK), (NZ, 24, RANK)]
-    + [(2, RANK, RANK), (RANK, RANK), (NX, 64, RANK), (NX - 1, 64, RANK), (NY, 8, RANK)]
-    + [(NY - 1, 8, RANK), (NX, NY, 8, RANK)]
+    + [(2, NZ, 32, RANK), (32, RANK), (NX, 8, RANK), (NX - 1, 8, RANK), (NY, 8, RANK)]
+    + [(NZ, NX, 8, RANK)]
     + [(2, RANK, RANK), (8, RANK), (NZ - 1, 8, RANK)]
 )
 HALF_SCRATCH = (
@@ -486,18 +524,19 @@
     + [(NX, 384, 48)] * 2
     + [(512, 192)] * 2
 )
-COPIES = 224
+COPIES = 232
 
 
 def finish(*refs):
-    sources, results, sems = refs[0:6], refs[6:12], refs[12]
-    copies = [
-        pltpu.make_async_copy(src, dst, sems.at[i])
-        for i, (src, dst) in enumerate(zip(sources, results))
-    ]
-    for copy in copies:
+    sources, results, held, sems = refs[0:6], refs[6:12], refs[12:18], refs[18]
+    reads = [pltpu.make_async_copy(a, b, sems.at[0, i]) for i, (a, b) in enumerate(zip(sources, held))]
+    writes = [pltpu.make_async_copy(a, b, sems.at[1, i]) for i, (a, b) in enumerate(zip(held, results))]
+    for copy in reads:
         copy.start()
-    for copy in copies:
+    for read, write in zip(reads, writes):
+        read.wait()
+        write.start()
+    for copy in writes:
         copy.wait()
 
 
@@ -524,7 +563,7 @@
         out_shape=out_shape,
         in_specs=[anywhere] * 6,
         out_specs=[anywhere] * 6,
-        scratch_shapes=[pltpu.SemaphoreType.DMA((6,))],
+        scratch_shapes=[pltpu.VMEM(s, F32) for s in shapes] + [pltpu.SemaphoreType.DMA((2, 6))],
     )(*results)
     return (*results[:5], jnp.swapaxes(results[5], 0, 1))
 

time: 143 us -> 99.7 us (0.70)
  Pallas kernels: 142 us -> 98.7 us
    pallas_call x1, Pallas kernels: 37.8 us -> 2.08 us  [body(): pl.pallas_call(finish, out_shape=out_shape, in_specs=[anywhere] * 6, out_...]
    pallas_call x1, Pallas kernels: 104 us -> 96.6 us  [body(): pl.pallas_call(kernel, out_shape=out_shape, in_specs=[anywhere, anywhere,...]
where the time goes in v3:
time: 99.7 us; the launch traced here: 99.5 us
  Pallas kernels  98.7 us (99%)
    pallas_call x1, Pallas kernels, body(): pl.pallas_call(kernel, out_shape=out_shape, in_specs=[anywhere, anywhere,...  96.6 us
    pallas_call x1, Pallas kernels, body(): pl.pallas_call(finish, out_shape=out_shape, in_specs=[anywhere] * 6, out_...  2.08 us

profile of v3, /device:TPU:1, one launch (start us, length us, event | category | flops | bytes accessed | tf_op | source)
XLA Modules:
  0.0 99.5 jit_solution(6884855912297064)
XLA Ops:
  0.6 96.6 %shard_map.109 = (f32[48,1536]{1,0:T(8,128)}, f32[48,1536]{1,0:T(8,128)}, f32[1,24,256]{2,1,0:T(8,128)}, f32[192,384]{1,0:T(8,128)}, f32[192,384]{1,0:T(8,128)}, /*index=5*/f32[6,1,256]{2,1,0:T(1,128)}) custom-call(f32[48,1536]{1,0:T(8,128)} %mom_up.1, bf16[48,1536]{1,0:T(8,128)(2,1)} %grad_up.1, f32[1,24,256]{2,1,0:T(8,128)} %basis_up.1, ...), custom_call_target="tpu_custom_call" | custom-call | tf_op jit(solution)/shard_map/pallas_call | solution.py:548
  97.2 2.1 %shard_map.110 = (f32[48,1536]{1,0:T(8,128)}, f32[48,1536]{1,0:T(8,128)}, f32[1,24,256]{2,1,0:T(8,128)}, f32[192,384]{1,0:T(8,128)}, f32[192,384]{1,0:T(8,128)}, /*index=5*/f32[6,1,256]{2,1,0:T(1,128)}) custom-call(f32[48,1536]{1,0:T(8,128)} %get-tuple-element.18.refs_0_, f32[48,1536]{1,0:T(8,128)} %get-tuple-element.19.refs_1_, ...), custom_call_target="tpu_custom_call" | custom-call | tf_op jit(solution)/shard_map/pallas_call | solution.py:561

commit v4 on v3

--- a/solution.py
+++ b/solution.py
@@ -90,7 +90,7 @@
     q, wfull, wpart, wcore, wsum, wu_x, wu_s, wu_y, wd_y, wd_s, wd_x,
     m_up, m_down, blend_up, blend_down, r_up, o_upd_up, o_new_up, o_upd_down, o_new_down,
     part_up, part_up_in, pfull_up, part_down, part_down_in, pfull_down,
-    gram, gram_in, gsum, g_x, g_y, g_all, xinv, ssum, ssum_in,
+    gram, gram_in, gsum, g_x, g_y, g_all, xinv, ssum, ssum_in, whole,
     g_up, g_down, bu_hi, bu_lo, pd_hi, pd_lo, tu_hi, tu_lo, td_hi, td_lo,
     send, recv, local,
 ):
@@ -129,95 +129,97 @@
     for load in loads:
         load.start()
 
-    started = []
-
-    def transfer(src, dst, device, arrives):
+    sent = [0] * PHASES
+    phase = [0]
+
+    def group(rows):
         n = count[0]
         count[0] += 1
-        copy = pltpu.make_async_remote_copy(
-            src, dst, send.at[n], recv.at[n], device_id=device, device_id_type=MESH
-        )
-        copy.start()
-        started.append(copy)
-        landing = pltpu.make_async_remote_copy(
-            src, arrives, send.at[n], recv.at[n], device_id=device, device_id_type=MESH
-        )
-        return landing.wait_recv
-
-    def wait(waits):
-        for w in waits:
-            w()
+
+        def arrive():
+            pltpu.make_async_remote_copy(
+                whole.at[0:rows], whole.at[0:rows], send.at[0], recv.at[n],
+                device_id=sibling, device_id_type=MESH,
+            ).wait_recv()
+
+        arrive.number = n
+        return arrive
+
+    def transfer(src, dst, device, to):
+        pltpu.make_async_remote_copy(
+            src, dst, send.at[phase[0]], recv.at[to.number], device_id=device, device_id_type=MESH
+        ).start()
+        sent[phase[0]] += math.prod(src.shape) // RANK
+
+    def drain(n):
+        pltpu.make_async_remote_copy(
+            whole.at[0 : sent[n]], whole.at[0 : sent[n]], send.at[n], recv.at[0],
+            device_id=sibling, device_id_type=MESH,
+        ).wait_send()
 
     def back(v, d, n):
         return lax.rem(v + n - d, n)
+
+    down_x = group(24)
+    down_y = group(224)
+    up_y = {d: group(24) for d in NEAR_FIRST}
+    up_x = {d: group(192) for d in range(1, NX)}
+    cores = [group(192) for _ in range(NX)] + [group(256)]
 
     class Gather:
         def __init__(self, buf):
             self.buf = buf
-            self.down_x = [
-                transfer(buf.at[x, y, c, 24:32], buf.at[x, y, c, 24:32], along_x(d),
-                         buf.at[back(x, d, NX), y, c, 24:32])
-                for d in range(1, NX)
-            ]
-            self.up_y = {
-                d: transfer(buf.at[x, y, c, 0:24], buf.at[x, y, c, 0:24], along_y(d),
-                            buf.at[x, back(y, d, NY), c, 0:24])
-                for d in NEAR_FIRST
-            }
-            self.up_x = {d: [] for d in range(1, NX)}
+            for d in (2, 1, 3):
+                piece = buf.at[x, y, c, 24:32]
+                transfer(piece, piece, along_x(d), down_x)
+            for d in NEAR_FIRST:
+                piece = buf.at[x, y, c, 0:24]
+                transfer(piece, piece, along_y(d), up_y[d])
             self.forward(y)
 
         def forward(self, yy):
             for d in (2, 1, 3):
                 piece = self.buf.at[x, yy, c, 0:24]
-                self.up_x[d].append(
-                    transfer(piece, piece, along_x(d), self.buf.at[back(x, d, NX), yy, c, 0:24])
-                )
+                transfer(piece, piece, along_x(d), up_x[d])
 
         def turn(self):
-            buf = self.buf
-            wait(self.down_x)
-            self.down_y = [
-                transfer(buf.at[:, y, c, 24:32], buf.at[:, y, c, 24:32], along_y(d),
-                         buf.at[:, back(y, d, NY), c, 24:32])
-                for d in FAR_FIRST
-            ]
+            down_x()
+            for d in FAR_FIRST:
+                piece = self.buf.at[:, y, c, 24:32]
+                transfer(piece, piece, along_y(d), down_y)
 
         def relay(self, *steps):
             for d in steps:
-                self.up_y[d]()
+                up_y[d]()
                 self.forward(back(y, d, NY))
 
         def own(self):
-            self.cores = {0: self.across(x)}
+            self.seen = [0]
+            self.across(0)
+
+        def across(self, d):
+            block = self.buf.at[back(x, d, NX), :, c, 0:24]
+            transfer(block, block, sibling, cores[d])
 
         def column(self, d):
-            wait(self.up_x[d])
-            self.cores[d] = self.across(back(x, d, NX))
-
-        def second(self):
-            self.turn()
-            self.relay(*NEAR_FIRST)
-            self.own()
-
-        def across(self, xx):
-            block = self.buf.at[xx, :, c, 0:24]
-            return transfer(block, block, sibling, self.buf.at[xx, :, 1 - c, 0:24])
+            up_x[d]()
+            self.seen.append(d)
+            self.across(d)
 
         def down(self):
-            wait(self.down_y)
+            down_y()
             block = self.buf.at[:, :, c, 24:32]
-            return transfer(block, block, sibling, self.buf.at[:, :, 1 - c, 24:32])
+            transfer(block, block, sibling, cores[NX])
 
         def up(self, use):
             before = 0
             for d in (1, 3, 2):
-                if d not in self.cores:
+                if d not in self.seen:
                     self.column(d)
-                self.cores[before]()
+                cores[before]()
                 use(back(x, before, NX))
                 before = d
-            self.cores[before]()
+            cores[before]()
             use(back(x, before, NX))
 
     q[x, y, c, 0:24, :] = basis_up[0]
@@ -238,113 +240,114 @@
         bu_hi[g], bu_lo[g] = halves(blend_up[:, 384 * g : 384 * g + 384])
     padded = dot(blend_down[...], pick)
     pd_hi[...], pd_lo[...] = halves(padded)
-    first.second()
-    first.down()()
+    first.turn()
+    first.relay(*NEAR_FIRST)
+    first.own()
+    first.down()
+    cores[NX]()
+    phase[0] = 1
 
     p_part = dot_halves(
         (pd_hi[...], pd_lo[...]), halves(q[:, :, :, 24:32, :].reshape(512, RANK))
     )
     part_down[...] = p_part.reshape(NZ, 24, RANK)
 
-    def reduce_z(part, part_in):
-        return [
-            transfer(part.at[lax.rem(z + d, NZ)], part_in.at[d - 1], along_z(d), part_in.at[d - 1])
-            for d in FAR_FIRST
-        ]
-
-    def gather_z(part, part_in, full):
+    def reduce_z(part, part_in, to):
+        for d in FAR_FIRST:
+            transfer(part.at[lax.rem(z + d, NZ)], part_in.at[d - 1], along_z(d), to)
+
+    def gather_z(part, part_in, full, to):
         total = part[z]
         for d in range(1, NZ):
             total = total + part_in[d - 1]
         full[z] = total
-        return [
-            transfer(full.at[z], full.at[z], along_z(d), full.at[back(z, d, NZ)])
-            for d in FAR_FIRST
-        ]
-
-    down_rs = reduce_z(part_down, part_down_in)
+        for d in FAR_FIRST:
+            transfer(full.at[z], full.at[z], along_z(d), to)
+
+    down_rs, down_ag, up_rs, up_ag = group(168), group(168), group(56), group(56)
+    reduce_z(part_down, part_down_in, down_rs)
+
     sums_up = []
 
     def add_up(g):
         piece = halves(q[g, :, :, 0:24, :].reshape(384, RANK))
         sums_up.append(dot_halves((bu_hi[g], bu_lo[g]), piece))
 
+    phase[0] = 0
     first.up(add_up)
+    phase[0] = 1
     part_up[0:6] = (sums_up[0] + sums_up[1] + sums_up[2] + sums_up[3]).reshape(6, 8, RANK)
     part_up[6:8] = jnp.zeros((2, 8, RANK), F32)
-    up_rs = reduce_z(part_up, part_up_in)
+    reduce_z(part_up, part_up_in, up_rs)
     for g in range(NX):
         tu_hi[g], tu_lo[g] = halves(blend_up[:, 384 * g : 384 * g + 384].T)
     td_hi[...], td_lo[...] = halves(padded.T)
-    wait(down_rs)
-    down_ag = gather_z(part_down, part_down_in, pfull_down)
-    wait(up_rs)
-    up_ag = gather_z(part_up, part_up_in, pfull_up)
-
-    wait(down_ag)
+    down_rs()
+    gather_z(part_down, part_down_in, pfull_down, down_ag)
+    up_rs()
+    gather_z(part_up, part_up_in, pfull_up, up_ag)
+
+    down_ag()
     p_down = pfull_down[...].reshape(192, RANK)
     gram[1] = dot(p_down, p_down, 0, 0).reshape(NZ, 32, RANK)
-    wait(up_ag)
+    up_ag()
     p_up = pfull_up[0:6].reshape(48, RANK)
     gram[0] = dot(p_up, p_up, 0, 0).reshape(NZ, 32, RANK)
-    gram_wait = transfer(gram.at[1 - c, z], gram_in, sibling, gram_in)
+    gram_core, gram_x, gram_y, gram_z, gram_all = [group(n) for n in (32, 24, 56, 56, 144)]
+    transfer(gram.at[1 - c, z], gram_in, sibling, gram_core)
     p_halves = halves(p_up)
-    core_up = {}
+    core_up = [group(192) for _ in range(NX)]
+    core_down = group(256)
+    w_x = [group(72) for _ in range(NY)]
+    w_y, wd_y_all, wd_x_all = group(168), group(224), group(24)
 
     def multiply(e):
         g = lax.rem(x + e, NX)
         wpart[g, :, :, 0:24, :] = dot_halves((tu_hi[g], tu_lo[g]), p_halves).reshape(
             NY, 2, 24, RANK
         )
-        core_up[e] = transfer(
-            wpart.at[g, :, 1 - c, 0:24], wcore.at[g, :, 0:24], sibling, wcore.at[g, :, 0:24]
-        )
+        phase[0] = 2
+        transfer(wpart.at[g, :, 1 - c, 0:24], wcore.at[g, :, 0:24], sibling, core_up[e])
+        phase[0] = 1
 
     def join(e):
         g = lax.rem(x + e, NX)
         core_up[e]()
         wsum[g, :, 0:24] = wpart[g, :, c, 0:24] + wcore[g, :, 0:24]
 
-    w_x = {d: [] for d in range(NY)}
-
     def scatter_x(e, d):
         yy = lax.rem(y + d, NY)
-        w_x[d].append(
-            transfer(wsum.at[lax.rem(x + e, NX), yy, 0:24], wu_x.at[e - 1, d], along_x(e),
-                     wu_x.at[e - 1, d])
-        )
-
-    w_y = []
+        phase[0] = 2
+        transfer(wsum.at[lax.rem(x + e, NX), yy, 0:24], wu_x.at[e - 1, d], along_x(e), w_x[d])
+        phase[0] = 1
 
     def scatter_y(d):
-        wait(w_x[d])
+        w_x[d]()
         wu_s[d] = wsum[x, lax.rem(y + d, NY), 0:24] + wu_x[0, d] + wu_x[1, d] + wu_x[2, d]
         if d:
-            w_y.append(transfer(wu_s.at[d], wu_y.at[d - 1], along_y(d), wu_y.at[d - 1]))
+            phase[0] = 2
+            transfer(wu_s.at[d], wu_y.at[d - 1], along_y(d), w_y)
+            phase[0] = 1
 
     multiply(2)
-    gram_wait()
+    gram_core()
     gsum[...] = (gram[c, z] + gram_in[...]).reshape(NX, 8, RANK)
-    gram_x = [
-        transfer(gsum.at[lax.rem(x + d, NX)], g_x.at[d - 1], along_x(d), g_x.at[d - 1])
-        for d in (2, 1, 3)
-    ]
+    for d in (2, 1, 3):
+        transfer(gsum.at[lax.rem(x + d, NX)], g_x.at[d - 1], along_x(d), gram_x)
     multiply(1)
     multiply(3)
     join(2)
     for d in FAR_FIRST + (0,):
         scatter_x(2, d)
-    wait(gram_x)
+    gram_x()
     g_y[y] = gsum[x] + g_x[0] + g_x[1] + g_x[2]
-    gram_y = [
-        transfer(g_y.at[y], g_y.at[y], along_y(d), g_y.at[back(y, d, NY)]) for d in FAR_FIRST
-    ]
+    for d in FAR_FIRST:
+        transfer(g_y.at[y], g_y.at[y], along_y(d), gram_y)
     wpart[:, :, :, 24:32, :] = dot_halves((td_hi[...], td_lo[...]), halves(p_down)).reshape(
         NX, NY, 2, 8, RANK
     )
-    core_down = transfer(
-        wpart.at[:, :, 1 - c, 24:32], wcore.at[:, :, 24:32], sibling, wcore.at[:, :, 24:32]
-    )
+    phase[0] = 2
+    transfer(wpart.at[:, :, 1 - c, 24:32], wcore.at[:, :, 24:32], sibling, core_down)
     join(1)
     join(3)
     for d in FAR_FIRST + (0,):
@@ -353,52 +356,45 @@
     multiply(0)
     core_down()
     wsum[:, :, 24:32] = wpart[:, :, c, 24:32] + wcore[:, :, 24:32]
-    down_y = [
-        transfer(wsum.at[:, lax.rem(y + d, NY), 24:32], wd_y.at[d - 1], along_y(d), wd_y.at[d - 1])
-        for d in FAR_FIRST
-    ]
+    phase[0] = 2
+    for d in FAR_FIRST:
+        transfer(wsum.at[:, lax.rem(y + d, NY), 24:32], wd_y.at[d - 1], along_y(d), wd_y_all)
+    phase[0] = 1
     join(0)
-    wait(gram_y)
+    gram_y()
     row = g_y[0]
     for i in range(1, NY):
         row = row + g_y[i]
     g_all[z, x] = row
-    gram_z = [
-        transfer(g_all.at[z, x], g_all.at[z, x], along_z(d), g_all.at[back(z, d, NZ), x])
-        for d in FAR_FIRST
-    ]
+    for d in FAR_FIRST:
+        transfer(g_all.at[z, x], g_all.at[z, x], along_z(d), gram_z)
     for d in FAR_FIRST[:3]:
         scatter_y(d)
-    wait(gram_z)
-    gram_x = []
+    gram_z()
     for d in (2, 1, 3):
-        xx = back(x, d, NX)
-        gram_x.append(transfer(g_all.at[0:4, x], g_all.at[0:4, x], along_x(d), g_all.at[0:4, xx]))
-        gram_x.append(
-            transfer(g_all.at[4:8, x, :, 128:256], g_all.at[4:8, x, :, 128:256], along_x(d),
-                     g_all.at[4:8, xx, :, 128:256])
-        )
+        for piece in (g_all.at[0:4, x], g_all.at[4:8, x, :, 128:256]):
+            transfer(piece, piece, along_x(d), gram_all)
     for d in FAR_FIRST[3:]:
         scatter_y(d)
-    wait(down_y)
+    wd_y_all()
     owned = wsum[:, y, 24:32]
     for d in range(1, NY):
         owned = owned + wd_y[d - 1]
     wd_s[...] = owned
-    down_x = [
-        transfer(wd_s.at[lax.rem(x + d, NX)], wd_x.at[d - 1], along_x(d), wd_x.at[d - 1])
-        for d in (2, 1, 3)
-    ]
+    phase[0] = 2
+    for d in (2, 1, 3):
+        transfer(wd_s.at[lax.rem(x + d, NX)], wd_x.at[d - 1], along_x(d), wd_x_all)
     scatter_y(0)
-    wait(w_y)
+    w_y()
     owned = wu_s[0]
     for d in range(1, NY):
         owned = owned + wu_y[d - 1]
     wfull[x, y, c, 0:24, :] = owned
-    wait(down_x)
+    wd_x_all()
     wfull[x, y, c, 24:32, :] = wd_s[x] + wd_x[0] + wd_x[1] + wd_x[2]
+    phase[0] = 3
     last = Gather(wfull)
-    wait(gram_x)
+    gram_all()
 
     g11, g12, g22 = (
         g_all[0:4, :, :, 0:128].reshape(128, 128),
@@ -429,11 +425,11 @@
 
     def hook(k):
         if k == 6:
-            late.append(last.down())
+            last.down()
         if k == 9:
             last.column(1)
         if k == 11:
-            late[0]()
+            cores[NX]()
             late.append(halves(dot(pick, wfull[:, :, :, 24:32, :].reshape(512, RANK))))
         if k == 12:
             last.column(3)
@@ -441,11 +437,14 @@
     x22 = invert_half(low, hook)
     xinv[c, 128:256, 128:256] = x22
     xinv[c, 128:256, 0:128] = -dot(x22, corner)
-    x_wait = transfer(xinv.at[c], xinv.at[c], sibling, xinv.at[1 - c])
+    x_wait = group(256)
+    phase[0] = 1
+    transfer(xinv.at[c], xinv.at[c], sibling, x_wait)
+    phase[0] = 3
     x_wait()
     x_up, x_down = halves(xinv[0]), halves(xinv[1])
 
-    right_down = dot_halves(late[1], x_down, 1, 1)
+    right_down = dot_halves(late[0], x_down, 1, 1)
     squares = []
 
     def turn(g):
@@ -457,9 +456,10 @@
     ssum[...] = jnp.zeros((8, RANK), F32)
     ssum[0:1, :] = squares[0] + squares[1] + squares[2] + squares[3]
     ssum[1:2, :] = jnp.sum(right_down * right_down, axis=0, keepdims=True)
-    s_wait = [
-        transfer(ssum, ssum_in.at[d - 1], along_z(d), ssum_in.at[d - 1]) for d in FAR_FIRST
-    ]
+    s_wait = group(56)
+    phase[0] = 4
+    for d in FAR_FIRST:
+        transfer(ssum, ssum_in.at[d - 1], along_z(d), s_wait)
     o_up = dot_halves(halves(p_up), x_up, 1, 1)
     o_down = dot_halves(halves(p_down), x_down, 1, 1)
     ou_halves, od_halves = halves(o_up), halves(o_down)
@@ -481,9 +481,9 @@
         )
     write(o_new_up, new_up)
     nb = dot_halves(halves(wfull[x, y, c, 24:32, :]), x_down, 1, 1)
-    while started:
-        started.pop().wait_send()
-    wait(s_wait)
+    for n in range(4):
+        drain(n)
+    s_wait()
     sums = ssum[...]
     for d in range(1, NZ):
         sums = sums + ssum_in[d - 1]
@@ -500,6 +500,7 @@
     nb = nb * s_down
     for i in range(6):
         nb_down[i] = nb[i : i + 1]
+    drain(4)
     for copy in writes:
         copy.wait()
 
@@ -515,7 +516,7 @@
     + [(NZ, 24, RANK), (NZ - 1, 24, RANK), (NZ, 24, RANK)]
     + [(2, NZ, 32, RANK), (32, RANK), (NX, 8, RANK), (NX - 1, 8, RANK), (NY, 8, RANK)]
     + [(NZ, NX, 8, RANK)]
-    + [(2, RANK, RANK), (8, RANK), (NZ - 1, 8, RANK)]
+    + [(2, RANK, RANK), (8, RANK), (NZ - 1, 8, RANK), (2048, RANK)]
 )
 HALF_SCRATCH = (
     [(48, 1536), (192, 384)]
@@ -524,7 +525,7 @@
     + [(NX, 384, 48)] * 2
     + [(512, 192)] * 2
 )
-COPIES = 232
+PHASES, GROUPS = 5, 56
 
 
 def finish(*refs):
@@ -552,7 +553,7 @@
         out_specs=[anywhere, anywhere, vmem] * 2,
         scratch_shapes=[pltpu.VMEM(s, F32) for s in SCRATCH]
         + [pltpu.VMEM(s, jnp.bfloat16) for s in HALF_SCRATCH]
-        + [pltpu.SemaphoreType.DMA((COPIES,))] * 2
+        + [pltpu.SemaphoreType.DMA((n,)) for n in (PHASES, GROUPS)]
         + [pltpu.SemaphoreType.DMA((8,))],
         compiler_params=pltpu.CompilerParams(
             collective_id=0, has_side_effects=True, vmem_limit_bytes=60 << 20

time: 99.7 us -> 96.7 us (0.970)
  Pallas kernels: 98.7 us -> 95.6 us
    pallas_call x1, Pallas kernels: 96.6 us -> 93.6 us  [body(): pl.pallas_call(kernel, out_shape=out_shape, in_specs=[anywhere, anywhere,...]
where the time goes in v4:
time: 96.7 us; the launch traced here: 96.5 us
  Pallas kernels  95.6 us (99%)
    pallas_call x1, Pallas kernels, body(): pl.pallas_call(kernel, out_shape=out_shape, in_specs=[anywhere, anywhere,...  93.6 us
    pallas_call x1, Pallas kernels, body(): pl.pallas_call(finish, out_shape=out_shape, in_specs=[anywhere] * 6, out_...  2.08 us

profile of v4, /device:TPU:1, one launch (start us, length us, event | category | flops | bytes accessed | tf_op | source)
XLA Modules:
  0.0 96.5 jit_solution(3344149151488124547)
XLA Ops:
  0.6 93.6 %shard_map.109 = (f32[48,1536]{1,0:T(8,128)}, f32[48,1536]{1,0:T(8,128)}, f32[1,24,256]{2,1,0:T(8,128)}, f32[192,384]{1,0:T(8,128)}, f32[192,384]{1,0:T(8,128)}, /*index=5*/f32[6,1,256]{2,1,0:T(1,128)}) custom-call(f32[48,1536]{1,0:T(8,128)} %mom_up.1, bf16[48,1536]{1,0:T(8,128)(2,1)} %grad_up.1, f32[1,24,256]{2,1,0:T(8,128)} %basis_up.1, ...), custom_call_target="tpu_custom_call" | custom-call | tf_op jit(solution)/shard_map/pallas_call | solution.py:549
  94.2 2.1 %shard_map.110 = (f32[48,1536]{1,0:T(8,128)}, f32[48,1536]{1,0:T(8,128)}, f32[1,24,256]{2,1,0:T(8,128)}, f32[192,384]{1,0:T(8,128)}, f32[192,384]{1,0:T(8,128)}, /*index=5*/f32[6,1,256]{2,1,0:T(1,128)}) custom-call(f32[48,1536]{1,0:T(8,128)} %get-tuple-element.18.refs_0_, f32[48,1536]{1,0:T(8,128)} %get-tuple-element.19.refs_1_, ...), custom_call_target="tpu_custom_call" | custom-call | tf_op jit(solution)/shard_map/pallas_call | solution.py:562

commit v5 on v4

--- a/solution.py
+++ b/solution.py
@@ -136,9 +136,9 @@
         n = count[0]
         count[0] += 1
 
-        def arrive():
+        def arrive(part=1):
             pltpu.make_async_remote_copy(
-                whole.at[0:rows], whole.at[0:rows], send.at[0], recv.at[n],
+                whole.at[0 : 2 * rows // part], whole.at[0 : 2 * rows // part], send.at[0], recv.at[n],
                 device_id=sibling, device_id_type=MESH,
             ).wait_recv()
 
@@ -149,7 +149,7 @@
         pltpu.make_async_remote_copy(
             src, dst, send.at[phase[0]], recv.at[to.number], device_id=device, device_id_type=MESH
         ).start()
-        sent[phase[0]] += math.prod(src.shape) // RANK
+        sent[phase[0]] += math.prod(src.shape) // 128
 
     def drain(n):
         pltpu.make_async_remote_copy(
@@ -162,25 +162,49 @@
 
     down_x = group(24)
     down_y = group(224)
-    up_y = {d: group(24) for d in NEAR_FIRST}
-    up_x = {d: group(192) for d in range(1, NX)}
-    cores = [group(192) for _ in range(NX)] + [group(256)]
-
-    class Gather:
+    up_y = [{d: group(24) for d in NEAR_FIRST} for _ in range(2)]
+    up_x = [{d: group(192) for d in range(1, NX)} for _ in range(2)]
+    cores = [[group(192) for _ in range(NX)] for _ in range(2)]
+    core_rest = group(256)
+
+    class Up:
+        def __init__(self, buf, lanes, half, part):
+            self.buf, self.lanes, self.part = buf, lanes, part
+            self.y, self.x, self.cores, self.seen = up_y[half], up_x[half], cores[half], []
+            for d in NEAR_FIRST:
+                piece = buf.at[x, y, c, 0:24, lanes]
+                transfer(piece, piece, along_y(d), self.y[d])
+            self.forward(y)
+
+        def forward(self, yy):
+            for d in (2, 1, 3):
+                piece = self.buf.at[x, yy, c, 0:24, self.lanes]
+                transfer(piece, piece, along_x(d), self.x[d])
+
+        def relay(self, *steps):
+            for d in steps:
+                self.y[d](self.part)
+                self.forward(back(y, d, NY))
+
+        def column(self, *steps):
+            for d in steps:
+                if d in self.seen:
+                    continue
+                if d:
+                    self.x[d](self.part)
+                self.seen.append(d)
+                block = self.buf.at[back(x, d, NX), :, c, 0:24, self.lanes]
+                transfer(block, block, sibling, self.cores[d])
+
+        def arrive(self, d):
+            self.cores[d](self.part)
+
+    class Down:
         def __init__(self, buf):
             self.buf = buf
             for d in (2, 1, 3):
                 piece = buf.at[x, y, c, 24:32]
                 transfer(piece, piece, along_x(d), down_x)
-            for d in NEAR_FIRST:
-                piece = buf.at[x, y, c, 0:24]
-                transfer(piece, piece, along_y(d), up_y[d])
-            self.forward(y)
-
-        def forward(self, yy):
-            for d in (2, 1, 3):
-                piece = self.buf.at[x, yy, c, 0:24]
-                transfer(piece, piece, along_x(d), up_x[d])
 
         def turn(self):
             down_x()
@@ -188,46 +212,31 @@
                 piece = self.buf.at[:, y, c, 24:32]
                 transfer(piece, piece, along_y(d), down_y)
 
-        def relay(self, *steps):
-            for d in steps:
-                up_y[d]()
-                self.forward(back(y, d, NY))
-
-        def own(self):
-            self.seen = [0]
-            self.across(0)
-
-        def across(self, d):
-            block = self.buf.at[back(x, d, NX), :, c, 0:24]
-            transfer(block, block, sibling, cores[d])
-
-        def column(self, d):
-            up_x[d]()
-            self.seen.append(d)
-            self.across(d)
-
-        def down(self):
+        def across(self):
             down_y()
             block = self.buf.at[:, :, c, 24:32]
-            transfer(block, block, sibling, cores[NX])
-
-        def up(self, use):
-            before = 0
-            for d in (1, 3, 2):
-                if d not in self.seen:
-                    self.column(d)
-                cores[before]()
-                use(back(x, before, NX))
-                before = d
-            cores[before]()
+            transfer(block, block, sibling, core_rest)
+
+    def collect(parts, use):
+        before = 0
+        for d in (1, 3, 2):
+            for part in parts:
+                part.column(d)
+            for part in parts:
+                part.arrive(before)
             use(back(x, before, NX))
+            before = d
+        for part in parts:
+            part.arrive(before)
+        use(back(x, before, NX))
 
     q[x, y, c, 0:24, :] = basis_up[0]
     q[x, y, c, 24:32, :] = jnp.zeros((8, RANK), F32)
     for i in range(6):
         q[x, y, c, 24 + i : 25 + i, :] = basis_down[i]
     pl.semaphore_wait(barrier, len(peers))
-    first = Gather(q)
+    first_down = Down(q)
+    first_up = Up(q, slice(0, RANK), 0, 1)
 
     column = lax.broadcasted_iota(jnp.int32, (384, 512), 0)
     slot = lax.broadcasted_iota(jnp.int32, (384, 512), 1)
@@ -240,11 +249,11 @@
         bu_hi[g], bu_lo[g] = halves(blend_up[:, 384 * g : 384 * g + 384])
     padded = dot(blend_down[...], pick)
     pd_hi[...], pd_lo[...] = halves(padded)
-    first.turn()
-    first.relay(*NEAR_FIRST)
-    first.own()
-    first.down()
-    cores[NX]()
+    first_down.turn()
+    first_up.relay(*NEAR_FIRST)
+    first_up.column(0)
+    first_down.across()
+    core_rest()
     phase[0] = 1
 
     p_part = dot_halves(
@@ -274,7 +283,7 @@
         sums_up.append(dot_halves((bu_hi[g], bu_lo[g]), piece))
 
     phase[0] = 0
-    first.up(add_up)
+    collect([first_up], add_up)
     phase[0] = 1
     part_up[0:6] = (sums_up[0] + sums_up[1] + sums_up[2] + sums_up[3]).reshape(6, 8, RANK)
     part_up[6:8] = jnp.zeros((2, 8, RANK), F32)
@@ -298,8 +307,10 @@
     p_halves = halves(p_up)
     core_up = [group(192) for _ in range(NX)]
     core_down = group(256)
-    w_x = [group(72) for _ in range(NY)]
-    w_y, wd_y_all, wd_x_all = group(168), group(224), group(24)
+    w_x = [[group(36) for _ in range(NY)] for _ in range(2)]
+    w_y = [group(84), group(84)]
+    wd_y_all, wd_x_all = group(224), group(24)
+    sides = [slice(0, 128), slice(128, 256)]
 
     def multiply(e):
         g = lax.rem(x + e, NX)
@@ -315,20 +326,39 @@
         core_up[e]()
         wsum[g, :, 0:24] = wpart[g, :, c, 0:24] + wcore[g, :, 0:24]
 
-    def scatter_x(e, d):
-        yy = lax.rem(y + d, NY)
+    def scatter_x(e, d, h):
         phase[0] = 2
-        transfer(wsum.at[lax.rem(x + e, NX), yy, 0:24], wu_x.at[e - 1, d], along_x(e), w_x[d])
+        transfer(
+            wsum.at[lax.rem(x + e, NX), lax.rem(y + d, NY), 0:24, sides[h]],
+            wu_x.at[e - 1, d, :, sides[h]], along_x(e), w_x[h][d],
+        )
         phase[0] = 1
 
-    def scatter_y(d):
-        w_x[d]()
-        wu_s[d] = wsum[x, lax.rem(y + d, NY), 0:24] + wu_x[0, d] + wu_x[1, d] + wu_x[2, d]
-        if d:
-            phase[0] = 2
-            transfer(wu_s.at[d], wu_y.at[d - 1], along_y(d), w_y)
-            phase[0] = 1
-
+    def scatter_y(h, *steps):
+        lanes = sides[h]
+        for d in steps:
+            w_x[h][d]()
+            wu_s[d, :, lanes] = (
+                wsum[x, lax.rem(y + d, NY), 0:24, lanes]
+                + wu_x[0, d, :, lanes] + wu_x[1, d, :, lanes] + wu_x[2, d, :, lanes]
+            )
+            if d:
+                phase[0] = 2
+                transfer(wu_s.at[d, :, lanes], wu_y.at[d - 1, :, lanes], along_y(d), w_y[h])
+                phase[0] = 1
+
+    def own_piece(h):
+        lanes = sides[h]
+        w_y[h]()
+        owned = wu_s[0, :, lanes]
+        for d in range(1, NY):
+            owned = owned + wu_y[d - 1, :, lanes]
+        wfull[x, y, c, 0:24, lanes] = owned
+        phase[0] = 3
+        gathers.append(Up(wfull, lanes, h, 2))
+        phase[0] = 1
+
+    gathers = []
     multiply(2)
     gram_core()
     gsum[...] = (gram[c, z] + gram_in[...]).reshape(NX, 8, RANK)
@@ -338,7 +368,8 @@
     multiply(3)
     join(2)
     for d in FAR_FIRST + (0,):
-        scatter_x(2, d)
+        scatter_x(2, d, 0)
+    multiply(0)
     gram_x()
     g_y[y] = gsum[x] + g_x[0] + g_x[1] + g_x[2]
     for d in FAR_FIRST:
@@ -351,9 +382,12 @@
     join(1)
     join(3)
     for d in FAR_FIRST + (0,):
-        scatter_x(1, d)
-        scatter_x(3, d)
-    multiply(0)
+        scatter_x(1, d, 0)
+        scatter_x(3, d, 0)
+    for d in FAR_FIRST + (0,):
+        scatter_x(2, d, 1)
+        scatter_x(1, d, 1)
+        scatter_x(3, d, 1)
     core_down()
     wsum[:, :, 24:32] = wpart[:, :, c, 24:32] + wcore[:, :, 24:32]
     phase[0] = 2
@@ -368,14 +402,12 @@
     g_all[z, x] = row
     for d in FAR_FIRST:
         transfer(g_all.at[z, x], g_all.at[z, x], along_z(d), gram_z)
-    for d in FAR_FIRST[:3]:
-        scatter_y(d)
+    scatter_y(0, *FAR_FIRST, 0)
+    scatter_y(1, *FAR_FIRST[:4])
     gram_z()
     for d in (2, 1, 3):
         for piece in (g_all.at[0:4, x], g_all.at[4:8, x, :, 128:256]):
             transfer(piece, piece, along_x(d), gram_all)
-    for d in FAR_FIRST[3:]:
-        scatter_y(d)
     wd_y_all()
     owned = wsum[:, y, 24:32]
     for d in range(1, NY):
@@ -384,16 +416,13 @@
     phase[0] = 2
     for d in (2, 1, 3):
         transfer(wd_s.at[lax.rem(x + d, NX)], wd_x.at[d - 1], along_x(d), wd_x_all)
-    scatter_y(0)
-    w_y()
-    owned = wu_s[0]
-    for d in range(1, NY):
-        owned = owned + wu_y[d - 1]
-    wfull[x, y, c, 0:24, :] = owned
+    phase[0] = 1
+    scatter_y(1, *FAR_FIRST[4:], 0)
+    own_piece(0)
     wd_x_all()
     wfull[x, y, c, 24:32, :] = wd_s[x] + wd_x[0] + wd_x[1] + wd_x[2]
     phase[0] = 3
-    last = Gather(wfull)
+    rest = Down(wfull)
     gram_all()
 
     g11, g12, g22 = (
@@ -403,16 +432,24 @@
     )
 
     def hook(k):
+        if k == 0:
+            own_piece(1)
+            phase[0] = 3
         if k == 1:
-            last.relay(1, 7)
-            last.turn()
+            gathers[0].relay(1, 7)
+        if k == 3:
+            gathers[0].relay(2, 6)
         if k == 5:
-            last.relay(2, 6)
-        if k == 9:
-            last.relay(3, 5)
-        if k == 12:
-            last.relay(4)
-            last.own()
+            rest.turn()
+        if k == 7:
+            gathers[1].relay(1, 7)
+        if k == 8:
+            gathers[0].relay(3, 5, 4)
+            gathers[0].column(0)
+        if k == 11:
+            gathers[1].relay(2, 6)
+        if k == 15:
+            gathers[1].relay(3, 5)
 
     x11 = invert_half(g11, hook)
     xinv[c, 0:128, 0:128] = x11
@@ -424,15 +461,17 @@
     late = []
 
     def hook(k):
-        if k == 6:
-            last.down()
-        if k == 9:
-            last.column(1)
+        if k == 0:
+            gathers[1].relay(4)
+            gathers[1].column(0)
+        if k == 4:
+            gathers[0].column(1, 3)
+        if k == 7:
+            gathers[0].column(2)
         if k == 11:
-            cores[NX]()
-            late.append(halves(dot(pick, wfull[:, :, :, 24:32, :].reshape(512, RANK))))
-        if k == 12:
-            last.column(3)
+            gathers[1].column(1, 3)
+        if k == 13:
+            rest.across()
 
     x22 = invert_half(low, hook)
     xinv[c, 128:256, 128:256] = x22
@@ -444,6 +483,8 @@
     x_wait()
     x_up, x_down = halves(xinv[0]), halves(xinv[1])
 
+    core_rest()
+    late.append(halves(dot(pick, wfull[:, :, :, 24:32, :].reshape(512, RANK))))
     right_down = dot_halves(late[0], x_down, 1, 1)
     squares = []
 
@@ -452,7 +493,7 @@
         r_up[g] = right
         squares.append(jnp.sum(right * right, axis=0, keepdims=True))
 
-    last.up(turn)
+    collect(gathers, turn)
     ssum[...] = jnp.zeros((8, RANK), F32)
     ssum[0:1, :] = squares[0] + squares[1] + squares[2] + squares[3]
     ssum[1:2, :] = jnp.sum(right_down * right_down, axis=0, keepdims=True)
@@ -516,7 +557,7 @@
     + [(NZ, 24, RANK), (NZ - 1, 24, RANK), (NZ, 24, RANK)]
     + [(2, NZ, 32, RANK), (32, RANK), (NX, 8, RANK), (NX - 1, 8, RANK), (NY, 8, RANK)]
     + [(NZ, NX, 8, RANK)]
-    + [(2, RANK, RANK), (8, RANK), (NZ - 1, 8, RANK), (2048, RANK)]
+    + [(2, RANK, RANK), (8, RANK), (NZ - 1, 8, RANK), (4096, 128)]
 )
 HALF_SCRATCH = (
     [(48, 1536), (192, 384)]
@@ -525,7 +566,7 @@
     + [(NX, 384, 48)] * 2
     + [(512, 192)] * 2
 )
-PHASES, GROUPS = 5, 56
+PHASES, GROUPS = 5, 80
 
 
 def finish(*refs):

time: 96.7 us -> 93.5 us (0.967)
  Pallas kernels: 95.6 us -> 92.5 us
    pallas_call x1, Pallas kernels: 93.6 us -> 90.4 us  [body(): pl.pallas_call(kernel, out_shape=out_shape, in_specs=[anywhere, anywhere,...]
where the time goes in v5:
time: 93.5 us; the launch traced here: 93.3 us
  Pallas kernels  92.5 us (99%)
    pallas_call x1, Pallas kernels, body(): pl.pallas_call(kernel, out_shape=out_shape, in_specs=[anywhere, anywhere,...  90.4 us
    pallas_call x1, Pallas kernels, body(): pl.pallas_call(finish, out_shape=out_shape, in_specs=[anywhere] * 6, out_...  2.08 us

profile of v5, /device:TPU:1, one launch (start us, length us, event | category | flops | bytes accessed | tf_op | source)
XLA Modules:
  0.0 93.3 jit_solution(6175845569644552014)
XLA Ops:
  0.6 90.4 %shard_map.109 = (f32[48,1536]{1,0:T(8,128)}, f32[48,1536]{1,0:T(8,128)}, f32[1,24,256]{2,1,0:T(8,128)}, f32[192,384]{1,0:T(8,128)}, f32[192,384]{1,0:T(8,128)}, /*index=5*/f32[6,1,256]{2,1,0:T(1,128)}) custom-call(f32[48,1536]{1,0:T(8,128)} %mom_up.1, bf16[48,1536]{1,0:T(8,128)(2,1)} %grad_up.1, f32[1,24,256]{2,1,0:T(8,128)} %basis_up.1, ...), custom_call_target="tpu_custom_call" | custom-call | tf_op jit(solution)/shard_map/pallas_call | solution.py:590
  91.1 2.1 %shard_map.110 = (f32[48,1536]{1,0:T(8,128)}, f32[48,1536]{1,0:T(8,128)}, f32[1,24,256]{2,1,0:T(8,128)}, f32[192,384]{1,0:T(8,128)}, f32[192,384]{1,0:T(8,128)}, /*index=5*/f32[6,1,256]{2,1,0:T(1,128)}) custom-call(f32[48,1536]{1,0:T(8,128)} %get-tuple-element.18.refs_0_, f32[48,1536]{1,0:T(8,128)} %get-tuple-element.19.refs_1_, ...), custom_call_target="tpu_custom_call" | custom-call | tf_op jit(solution)/shard_map/pallas_call | solution.py:603

commit v6 on v5

--- a/solution.py
+++ b/solution.py
@@ -88,10 +88,10 @@
     mom_up, grad_up, basis_up, mom_down, grad_down, basis_down,
     upd_up, new_up, nb_up, upd_down, new_down, nb_down,
     q, wfull, wpart, wcore, wsum, wu_x, wu_s, wu_y, wd_y, wd_s, wd_x,
-    m_up, m_down, blend_up, blend_down, r_up, o_upd_up, o_new_up, o_upd_down, o_new_down,
+    m_up, m_down, blend_up, blend_down, o_upd_up, o_new_up, o_upd_down, o_new_down,
     part_up, part_up_in, pfull_up, part_down, part_down_in, pfull_down,
-    gram, gram_in, gsum, g_x, g_y, g_all, xinv, ssum, ssum_in, whole,
-    g_up, g_down, bu_hi, bu_lo, pd_hi, pd_lo, tu_hi, tu_lo, td_hi, td_lo,
+    turned_up, turned_down, gram, gram_in, gsum, g_x, g_y, g_all, xinv, ssum, ssum_in, whole,
+    g_up, g_down, bu_hi, bu_lo, pd_hi, pd_lo, tu_hi, tu_lo, td_hi, td_lo, wd_half,
     send, recv, local,
 ):
     x, y, c, z = place()
@@ -116,6 +116,7 @@
         [along_y(d) for d in range(1, NY)]
         + [along_x(d) for d in range(1, NX)]
         + [along_z(d) for d in range(1, NZ)]
+        + [at(x, y, 1 - c, lax.rem(z + d, NZ)) for d in range(1, NZ)]
         + [sibling]
     )
     for peer in peers:
@@ -298,12 +299,15 @@
 
     down_ag()
     p_down = pfull_down[...].reshape(192, RANK)
-    gram[1] = dot(p_down, p_down, 0, 0).reshape(NZ, 32, RANK)
+    rows = pl.ds(pl.multiple_of(32 * z, 8), 32)
+    turned_down[...] = p_down.T
+    gram[1] = dot(turned_down[rows, :], p_down)
     up_ag()
     p_up = pfull_up[0:6].reshape(48, RANK)
-    gram[0] = dot(p_up, p_up, 0, 0).reshape(NZ, 32, RANK)
+    turned_up[...] = p_up.T
+    gram[0] = dot(turned_up[rows, :], p_up)
     gram_core, gram_x, gram_y, gram_z, gram_all = [group(n) for n in (32, 24, 56, 56, 144)]
-    transfer(gram.at[1 - c, z], gram_in, sibling, gram_core)
+    transfer(gram.at[1 - c], gram_in, sibling, gram_core)
     p_halves = halves(p_up)
     core_up = [group(192) for _ in range(NX)]
     core_down = group(256)
@@ -361,7 +365,7 @@
     gathers = []
     multiply(2)
     gram_core()
-    gsum[...] = (gram[c, z] + gram_in[...]).reshape(NX, 8, RANK)
+    gsum[...] = (gram[c] + gram_in[...]).reshape(NX, 8, RANK)
     for d in (2, 1, 3):
         transfer(gsum.at[lax.rem(x + d, NX)], g_x.at[d - 1], along_x(d), gram_x)
     multiply(1)
@@ -480,31 +484,39 @@
     phase[0] = 1
     transfer(xinv.at[c], xinv.at[c], sibling, x_wait)
     phase[0] = 3
+    core_rest()
+    select = pick.astype(jnp.bfloat16)
+    for i, half in enumerate(halves(wfull[:, :, :, 24:32, :].reshape(512, RANK))):
+        rows = lax.dot_general(
+            select, half, (((1,), (0,)), ((), ())), preferred_element_type=F32
+        )
+        wd_half[i] = rows.astype(jnp.bfloat16).reshape(2, 192, RANK)
     x_wait()
     x_up, x_down = halves(xinv[0]), halves(xinv[1])
-
-    core_rest()
-    late.append(halves(dot(pick, wfull[:, :, :, 24:32, :].reshape(512, RANK))))
-    right_down = dot_halves(late[0], x_down, 1, 1)
-    squares = []
-
-    def turn(g):
-        right = dot_halves(halves(wfull[g, :, :, 0:24, :].reshape(384, RANK)), x_up, 1, 1)
-        r_up[g] = right
-        squares.append(jnp.sum(right * right, axis=0, keepdims=True))
-
-    collect(gathers, turn)
+    right = dot_halves((wd_half[0, c], wd_half[1, c]), x_down, 1, 1)
+    sum_down = jnp.sum(right * right, axis=0, keepdims=True)
+    collect(gathers, lambda g: None)
+    sum_up = jnp.zeros((1, RANK), F32)
+    for i in range(2):
+        w = halves(wfull[back(x, 2 * i + c, NX), :, :, 0:24, :].reshape(384, RANK))
+        right = dot_halves(w, x_up, 1, 1)
+        sum_up = sum_up + jnp.sum(right * right, axis=0, keepdims=True)
     ssum[...] = jnp.zeros((8, RANK), F32)
-    ssum[0:1, :] = squares[0] + squares[1] + squares[2] + squares[3]
-    ssum[1:2, :] = jnp.sum(right_down * right_down, axis=0, keepdims=True)
-    s_wait = group(56)
+    ssum[0:1, :] = sum_up
+    ssum[1:2, :] = sum_down
+    s_wait = group(120)
     phase[0] = 4
-    for d in FAR_FIRST:
-        transfer(ssum, ssum_in.at[d - 1], along_z(d), s_wait)
+    for d in FAR_FIRST + (0,):
+        zz = lax.rem(z + d, NZ)
+        transfer(ssum, ssum_in.at[8 * c + d], at(x, y, 1 - c, zz), s_wait)
+        if d:
+            transfer(ssum, ssum_in.at[8 * c + d], at(x, y, c, zz), s_wait)
+    ssum_in[8 * c] = ssum[...]
     o_up = dot_halves(halves(p_up), x_up, 1, 1)
     o_down = dot_halves(halves(p_down), x_down, 1, 1)
-    ou_halves, od_halves = halves(o_up), halves(o_down)
-    rd_halves = halves(right_down)
+    z_up = halves(dot_halves(halves(o_up), x_up))
+    z_down = halves(dot_halves(halves(o_down), x_down))
+    wd_all = (wd_half[0].reshape(384, RANK), wd_half[1].reshape(384, RANK))
     writes = []
 
     def write(src, dst):
@@ -512,32 +524,34 @@
         copy.start()
         writes.append(copy)
 
-    o_new_down[...] = blend_down[...] - (1.0 - retain) * dot_halves(od_halves, rd_halves, 1, 1)
+    o_new_down[...] = blend_down[...] - (1.0 - retain) * dot_halves(z_down, wd_all, 1, 1)
     write(o_new_down, new_down)
-    ru_halves = [halves(r_up[g]) for g in range(NX)]
+    w_halves = []
     for g in range(NX):
         cols = slice(384 * g, 384 * g + 384)
+        w_halves.append(halves(wfull[g, :, :, 0:24, :].reshape(384, RANK)))
         o_new_up[:, cols] = blend_up[:, cols] - (1.0 - retain) * dot_halves(
-            ou_halves, ru_halves[g], 1, 1
+            z_up, w_halves[g], 1, 1
         )
     write(o_new_up, new_up)
+    nb_one = dot_halves(halves(wfull[x, y, c, 0:24, :]), x_up, 1, 1)
     nb = dot_halves(halves(wfull[x, y, c, 24:32, :]), x_down, 1, 1)
     for n in range(4):
         drain(n)
     s_wait()
-    sums = ssum[...]
-    for d in range(1, NZ):
-        sums = sums + ssum_in[d - 1]
+    sums = ssum_in[0]
+    for i in range(1, 16):
+        sums = sums + ssum_in[i]
     scale = lax.rsqrt(sums + epsilon)
     s_up, s_down = scale[0:1], scale[1:2]
-    ou_halves = halves(math.sqrt(3072 / 12288) * o_up * s_up)
+    z_up = halves(dot_halves(halves(math.sqrt(3072 / 12288) * o_up * s_up), x_up))
     for g in range(NX):
-        o_upd_up[:, 384 * g : 384 * g + 384] = dot_halves(ou_halves, ru_halves[g], 1, 1)
+        o_upd_up[:, 384 * g : 384 * g + 384] = dot_halves(z_up, w_halves[g], 1, 1)
     write(o_upd_up, upd_up)
-    od_halves = halves(math.sqrt(12288 / 3072) * o_down * s_down)
-    o_upd_down[...] = dot_halves(od_halves, rd_halves, 1, 1)
+    z_down = halves(dot_halves(halves(math.sqrt(12288 / 3072) * o_down * s_down), x_down))
+    o_upd_down[...] = dot_halves(z_down, wd_all, 1, 1)
     write(o_upd_down, upd_down)
-    nb_up[0] = r_up[x, pl.ds(pl.multiple_of(48 * y + 24 * c, 8), 24), :] * s_up
+    nb_up[0] = nb_one * s_up
     nb = nb * s_down
     for i in range(6):
         nb_down[i] = nb[i : i + 1]
@@ -551,13 +565,13 @@
     [PIECES, PIECES, PIECES, (NX, NY, 32, RANK), (NX, NY, 32, RANK)]
     + [(NX - 1, NY, 24, RANK), (NY, 24, RANK), (NY - 1, 24, RANK)]
     + [(NY - 1, NX, 8, RANK), (NX, 8, RANK), (NX - 1, 8, RANK)]
-    + [(48, 1536), (192, 384), (48, 1536), (192, 384), (NX, 384, RANK)]
+    + [(48, 1536), (192, 384), (48, 1536), (192, 384)]
     + [(48, 1536), (48, 1536), (192, 384), (192, 384)]
     + [(NZ, 8, RANK), (NZ - 1, 8, RANK), (NZ, 8, RANK)]
     + [(NZ, 24, RANK), (NZ - 1, 24, RANK), (NZ, 24, RANK)]
-    + [(2, NZ, 32, RANK), (32, RANK), (NX, 8, RANK), (NX - 1, 8, RANK), (NY, 8, RANK)]
+    + [(RANK, 48), (RANK, 192), (2, 32, RANK), (32, RANK), (NX, 8, RANK), (NX - 1, 8, RANK), (NY, 8, RANK)]
     + [(NZ, NX, 8, RANK)]
-    + [(2, RANK, RANK), (8, RANK), (NZ - 1, 8, RANK), (4096, 128)]
+    + [(2, RANK, RANK), (8, RANK), (16, 8, RANK), (4096, 128)]
 )
 HALF_SCRATCH = (
     [(48, 1536), (192, 384)]
@@ -565,6 +579,7 @@
     + [(192, 512)] * 2
     + [(NX, 384, 48)] * 2
     + [(512, 192)] * 2
+    + [(2, 2, 192, RANK)]
 )
 PHASES, GROUPS = 5, 80
 

time: 93.5 us -> 92.5 us (0.989)
  no operation moved by 1% of the time
where the time goes in v6:
time: 92.5 us; the launch traced here: 92.3 us
  Pallas kernels  91.6 us (99%)
    pallas_call x1, Pallas kernels, body(): pl.pallas_call(kernel, out_shape=out_shape, in_specs=[anywhere, anywhere,...  89.6 us
    pallas_call x1, Pallas kernels, body(): pl.pallas_call(finish, out_shape=out_shape, in_specs=[anywhere] * 6, out_...  2.08 us

profile of v6, /device:TPU:1, one launch (start us, length us, event | category | flops | bytes accessed | tf_op | source)
XLA Modules:
  0.0 92.3 jit_solution(13409208108291802286)
XLA Ops:
  0.6 89.6 %shard_map.109 = (f32[48,1536]{1,0:T(8,128)}, f32[48,1536]{1,0:T(8,128)}, f32[1,24,256]{2,1,0:T(8,128)}, f32[192,384]{1,0:T(8,128)}, f32[192,384]{1,0:T(8,128)}, /*index=5*/f32[6,1,256]{2,1,0:T(1,128)}) custom-call(f32[48,1536]{1,0:T(8,128)} %mom_up.1, bf16[48,1536]{1,0:T(8,128)(2,1)} %grad_up.1, f32[1,24,256]{2,1,0:T(8,128)} %basis_up.1, ...), custom_call_target="tpu_custom_call" | custom-call | tf_op jit(solution)/shard_map/pallas_call | solution.py:605
  90.2 2.1 %shard_map.110 = (f32[48,1536]{1,0:T(8,128)}, f32[48,1536]{1,0:T(8,128)}, f32[1,24,256]{2,1,0:T(8,128)}, f32[192,384]{1,0:T(8,128)}, f32[192,384]{1,0:T(8,128)}, /*index=5*/f32[6,1,256]{2,1,0:T(1,128)}) custom-call(f32[48,1536]{1,0:T(8,128)} %get-tuple-element.18.refs_0_, f32[48,1536]{1,0:T(8,128)} %get-tuple-element.19.refs_1_, ...), custom_call_target="tpu_custom_call" | custom-call | tf_op jit(solution)/shard_map/pallas_call | solution.py:618

commit v7 on v6

--- a/solution.py
+++ b/solution.py
@@ -254,6 +254,14 @@
     first_up.relay(*NEAR_FIRST)
     first_up.column(0)
     first_down.across()
+    sums_up = []
+
+    def add_up(g):
+        piece = halves(q[g, :, :, 0:24, :].reshape(384, RANK))
+        sums_up.append(dot_halves((bu_hi[g], bu_lo[g]), piece))
+
+    first_up.arrive(0)
+    add_up(x)
     core_rest()
     phase[0] = 1
 
@@ -277,14 +285,14 @@
     down_rs, down_ag, up_rs, up_ag = group(168), group(168), group(56), group(56)
     reduce_z(part_down, part_down_in, down_rs)
 
-    sums_up = []
-
-    def add_up(g):
-        piece = halves(q[g, :, :, 0:24, :].reshape(384, RANK))
-        sums_up.append(dot_halves((bu_hi[g], bu_lo[g]), piece))
-
     phase[0] = 0
-    collect([first_up], add_up)
+    first_up.column(1, 3)
+    for d in (1, 3):
+        first_up.arrive(d)
+        add_up(back(x, d, NX))
+    first_up.column(2)
+    first_up.arrive(2)
+    add_up(back(x, 2, NX))
     phase[0] = 1
     part_up[0:6] = (sums_up[0] + sums_up[1] + sums_up[2] + sums_up[3]).reshape(6, 8, RANK)
     part_up[6:8] = jnp.zeros((2, 8, RANK), F32)
@@ -436,21 +444,21 @@
     )
 
     def hook(k):
-        if k == 0:
+        if k == 2:
             own_piece(1)
             phase[0] = 3
-        if k == 1:
+        if k == 3:
             gathers[0].relay(1, 7)
-        if k == 3:
+        if k == 5:
             gathers[0].relay(2, 6)
-        if k == 5:
+        if k == 7:
             rest.turn()
-        if k == 7:
+        if k == 9:
             gathers[1].relay(1, 7)
-        if k == 8:
+        if k == 10:
             gathers[0].relay(3, 5, 4)
             gathers[0].column(0)
-        if k == 11:
+        if k == 13:
             gathers[1].relay(2, 6)
         if k == 15:
             gathers[1].relay(3, 5)

time: 92.5 us -> 93.2 us (level)
  no operation moved by 1% of the time
where the time goes in v7:
time: 93.2 us; the launch traced here: 93 us
  Pallas kernels  92.4 us (99%)
    pallas_call x1, Pallas kernels, body(): pl.pallas_call(kernel, out_shape=out_shape, in_specs=[anywhere, anywhere,...  90.3 us
    pallas_call x1, Pallas kernels, body(): pl.pallas_call(finish, out_shape=out_shape, in_specs=[anywhere] * 6, out_...  2.08 us

profile of v7, /device:TPU:1, one launch (start us, length us, event | category | flops | bytes accessed | tf_op | source)
XLA Modules:
  0.0 93.0 jit_solution(13226183243195572749)
XLA Ops:
  0.6 90.3 %shard_map.109 = (f32[48,1536]{1,0:T(8,128)}, f32[48,1536]{1,0:T(8,128)}, f32[1,24,256]{2,1,0:T(8,128)}, f32[192,384]{1,0:T(8,128)}, f32[192,384]{1,0:T(8,128)}, /*index=5*/f32[6,1,256]{2,1,0:T(1,128)}) custom-call(f32[48,1536]{1,0:T(8,128)} %mom_up.1, bf16[48,1536]{1,0:T(8,128)(2,1)} %grad_up.1, f32[1,24,256]{2,1,0:T(8,128)} %basis_up.1, ...), custom_call_target="tpu_custom_call" | custom-call | tf_op jit(solution)/shard_map/pallas_call | solution.py:613
  90.9 2.1 %shard_map.110 = (f32[48,1536]{1,0:T(8,128)}, f32[48,1536]{1,0:T(8,128)}, f32[1,24,256]{2,1,0:T(8,128)}, f32[192,384]{1,0:T(8,128)}, f32[192,384]{1,0:T(8,128)}, /*index=5*/f32[6,1,256]{2,1,0:T(1,128)}) custom-call(f32[48,1536]{1,0:T(8,128)} %get-tuple-element.18.refs_0_, f32[48,1536]{1,0:T(8,128)} %get-tuple-element.19.refs_1_, ...), custom_call_target="tpu_custom_call" | custom-call | tf_op jit(solution)/shard_map/pallas_call | solution.py:626
